TPU v7x, 128 devices: a whole 4x4x4 slice. The times are simulated.
128 devices in a mesh: row: 16 (over y, x_hi, core), col: 8 (over z, x_lo).
Axes of the slice: x: 4 (x_hi: 2, x_lo: 2; x = x_hi * 2 + x_lo), y: 4, z: 4, core: 2. Of those that a mesh axis runs over, the one named last changes fastest.
Arguments:
- x_act: bfloat16 [4096, 7168], P(('row', 'col')), may hold values from -0.09375 to 0.09375
- grad_out: bfloat16 [4096, 28672], P('col', 'row'), may hold values from -6 to 6
- weight: bfloat16 [7168, 28672], P('col', 'row'), may hold values from -0.078125 to 0.078125
- block_mask: int32 [56, 224], P('col', 'row'), may hold values from 0 to 1, as said below
Outputs:
- grad_in: bfloat16 [4096, 7168], P('row', 'col')
- grad_weight: bfloat16 [7168, 28672], P('col', 'row')
Inputs may be any that keep to these rules, and one draw needn't show every extreme that they name: `block_mask`: the tile of 7 x 14 blocks that one device holds has at most 26 live blocks, and some tile has exactly 26; every tile has at least half of 26.
All inputs are finite; a program needn't handle non-finite values.
Results may differ from a plain program's by a relative error of at most 0.011.
Values may be sent and summed in bfloat16 or wider, within the bound.
No kernel may reach another device: no remote copies, remote signals or barrier semaphores. Data moves between devices by JAX's collectives and lax.ppermute only.
A program may use at most 128 MiB of HBM per device.

v0:
```python
import math

import jax
import jax.numpy as jnp
from jax import lax
from jax.sharding import PartitionSpec as P


def on_device(x_act, grad_out, weight, block_mask):
    dblk, fblk = block_mask.shape
    blk = weight.shape[0] // dblk
    count_all = dblk * fblk
    cap = count_all * 4 // 15
    flat = block_mask.reshape(-1)
    places = jnp.arange(count_all, dtype=jnp.int32)
    order = jnp.argsort((1 - flat) * count_all + places)
    picked = order[:cap]
    onehot = (picked[:, None] == places[None, :]).astype(jnp.int32)
    valid = jnp.sum(onehot * flat[None, :], axis=1).astype(jnp.float32)
    pick_d = ((picked // fblk)[:, None] == jnp.arange(dblk, dtype=jnp.int32)[None, :]).astype(
        jnp.float32
    )
    pick_f = ((picked % fblk)[:, None] == jnp.arange(fblk, dtype=jnp.int32)[None, :]).astype(
        jnp.float32
    )
    pick_d_half = pick_d.astype(jnp.bfloat16)
    pick_f_half = pick_f.astype(jnp.bfloat16)
    weight4 = weight.reshape(dblk, blk, fblk, blk)
    row_pick = jnp.einsum(
        "ibje,ci->cbje", weight4, pick_d_half, preferred_element_type=jnp.float32
    ).astype(jnp.bfloat16)
    live_w = jnp.einsum("cbje,cj->cbe", row_pick, pick_f_half, preferred_element_type=jnp.float32)
    live_w = (live_w * valid[:, None, None]).astype(jnp.bfloat16)
    weight_init = jnp.zeros((cap, blk, blk), jnp.float32)

    def select_grads(grows):
        rows = grows.shape[0]
        return jnp.einsum(
            "kjb,cj->kcb",
            grows.reshape(rows, fblk, blk),
            pick_f_half,
            preferred_element_type=jnp.float32,
        ).astype(jnp.bfloat16)

    def weight_term(xrows, chosen):
        rows = xrows.shape[0]
        xsel = jnp.einsum(
            "kib,ci->kcb",
            xrows.reshape(rows, dblk, blk),
            pick_d_half,
            preferred_element_type=jnp.float32,
        ).astype(jnp.bfloat16)
        return jnp.einsum("kcb,kce->cbe", xsel, chosen, preferred_element_type=jnp.float32)

    def input_term(grows, chosen):
        rows = grows.shape[0]
        partial_blocks = jnp.einsum(
            "kce,cbe->kcb", chosen, live_w, preferred_element_type=jnp.float32
        )
        high_part = partial_blocks.astype(jnp.bfloat16)
        low_part = (partial_blocks - high_part.astype(jnp.float32)).astype(jnp.bfloat16)
        placed = jnp.einsum(
            "kcb,ci->kib", high_part, pick_d_half, preferred_element_type=jnp.float32
        )
        placed = placed + jnp.einsum(
            "kcb,ci->kib", low_part, pick_d_half, preferred_element_type=jnp.float32
        )
        return placed.reshape(rows, dblk * blk)

    def picked_grads(grows):
        return select_grads(grows)

    x_local = lax.all_to_all(x_act, "col", split_axis=1, concat_axis=0, tiled=True)
    x_full = lax.all_gather(x_local, "row", axis=0, tiled=True)
    tokens = x_full.shape[0]
    feat = x_full.shape[1]
    empty_dx = jnp.zeros((tokens, feat), jnp.float32)
    piece = lax.all_gather(grad_out, "col", axis=0, tiled=True)
    count = piece.shape[0]
    sub = math.gcd(count, 512)

    def step(turn, inner):
        wsum, xsum = inner
        offset = turn * sub
        grows = lax.dynamic_slice_in_dim(piece, offset, sub, 0)
        xrows = lax.dynamic_slice_in_dim(x_full, offset, sub, 0)
        chosen = picked_grads(grows)
        wsum = wsum + weight_term(xrows, chosen)
        xsum = lax.dynamic_update_slice_in_dim(xsum, input_term(grows, chosen), offset, 0)
        return (wsum, xsum)

    weight_sum, input_sum = lax.fori_loop(0, count // sub, step, (weight_init, empty_dx))
    grad_in = lax.psum_scatter(input_sum, "row", scatter_dimension=0, tiled=True).astype(
        jnp.bfloat16
    )
    spread = jnp.einsum(
        "cbe,ci->icbe", weight_sum * valid[:, None, None], pick_d, precision=lax.Precision.HIGHEST
    )
    placed = jnp.einsum("icbe,cj->ibje", spread, pick_f, precision=lax.Precision.HIGHEST)
    return (grad_in, placed.reshape(weight.shape).astype(jnp.bfloat16))


def solution(mesh):
    placed = (P(("row", "col"), None), P("col", "row"), P("col", "row"), P("col", "row"))
    return jax.shard_map(
        on_device,
        mesh=mesh,
        in_specs=placed,
        out_specs=(P("row", "col"), P("col", "row")),
        check_vma=False,
    )
```

profile of v0, /device:TPU:26, one launch (start us, length us, event | category | flops | bytes accessed | tf_op | source)
XLA Modules:
  0.0 773.0 jit_solution(322660678393857667)
XLA Ops:
  8.3 15.2 %all_to_all.19 = bf16[32,8,896]{2,0,1:T(8,128)(2,1)} all-to-all(bf16[32,8,896]{2,0,1:T(8,128)(2,1)S(1)} %bitcast.93), channel_id=1, replica_groups=mesh['row'=16,'col'=8] {'col'}, dimensions={1} | all-to-all | bytes 917504 | tf_op jit(solution)/shard_map/all_to_all | solution.py:73
  23.5 3.8 copy.72
  27.5 2.6 sort.17
  30.4 3.8 reshape.44
  34.2 5.8 convolution_convert_fusion
  40.0 14.3 %fusion.33 = f32[26,1,128,128]{3,1,2,0:T(1,128)S(1)} fusion(bf16[26,14,1,1]{1,2,3,0:T(2,128)(2,1)S(1)} %copy.79, bf16[26,128,14,128]{3,0,2,1:T(8,128)(2,1)S(1)} %convolution_convert_fusion), kind=kOutput, calls=%fused_computation.34 | convolution fusion | flops 11927552 | bytes 13632216 | tf_op jit(solution)/shard_map/cbje,cj->cbe/dot_general | solution.py:32
  55.4 33.4 %all-gather.3.cloned.1.call-done = bf16[4096,896]{1,0:T(8,128)(2,1)} async-done(((bf16[256,896]{1,0:T(8,128)(2,1)}), bf16[4096,896]{1,0:T(8,128)(2,1)}) %all-gather.3.cloned.1.call-update) | async-done | bytes 7340048 | tf_op jit(solution)/shard_map/all_gather | solution.py:74
  88.8 289.3 %all-gather.5.cloned.1.call-done = bf16[4096,1792]{0,1:T(8,128)(2,1)} async-done(((bf16[512,1792]{0,1:T(8,128)(2,1)}), bf16[4096,1792]{0,1:T(8,128)(2,1)}) %all-gather.5.cloned.1.call-update) | async-done | bytes 14680080 | tf_op jit(solution)/shard_map/all_gather | solution.py:78
  378.1 6.1 broadcast_in_dim.5.clone
  384.2 248.6 %while.16 = (s32[]{:T(128)}, f32[26,128,128]{2,1,0:T(8,128)}, f32[4096,896]{1,0:T(8,128)}, bf16[4096,896]{1,0:T(8,128)(2,1)}, bf16[4096,1792]{0,1:T(8,128)(2,1)}...) while((s32[]{:T(128)}, f32[26,128,128]{2,1,0:T(8,128)}, ...), condition=%wide.region_3.4_spmd.clone, body=%wide.region_2.3_spmd.clone.sunk | while | flops 1003227904 | bytes 70451832 | solution.py:92
  387.2 2.9 constant_dynamic-slice_fusion.4
  390.0 3.4 copy.128
  396.0 7.1 select_add_fusion.2
  403.1 2.3 fusion.78
  416.9 2.9 constant_dynamic-slice_fusion.4
  419.7 3.4 copy.128
  425.7 8.6 %select_add_fusion.2 = f32[26,128,128]{2,1,0:T(8,128)} fusion(f32[26,128,128]{2,1,0:T(8,128)} %get-tuple-element.298, bf16[512,26,128]{2,1,0:T(8,128)(2,1)S(1)} %convert_bitcast_fusion.4, bf16[512,26,128]{2,1,0:T(8,128)(2,1)S(1)} %convert_bitcast_fusion.5, pred[]{:T(512)S(6)} %compare.7), kind=kOutput, calls=%fused_computation.17.clone.1 | convolution fusion | flops 437059584 | bytes 10223617 | tf_op jit(solution)/shard_map/while/body/eval_jaxpr/kcb,kce->cbe/dot_general | solution.py:53
  434.3 2.3 fusion.78
  448.1 2.9 constant_dynamic-slice_fusion.4
  450.9 3.4 copy.128
  456.9 8.6 %select_add_fusion.2 = f32[26,128,128]{2,1,0:T(8,128)} fusion(f32[26,128,128]{2,1,0:T(8,128)} %get-tuple-element.298, bf16[512,26,128]{2,1,0:T(8,128)(2,1)S(1)} %convert_bitcast_fusion.4, bf16[512,26,128]{2,1,0:T(8,128)(2,1)S(1)} %convert_bitcast_fusion.5, pred[]{:T(512)S(6)} %compare.7), kind=kOutput, calls=%fused_computation.17.clone.1 | convolution fusion | flops 437059584 | bytes 10223617 | tf_op jit(solution)/shard_map/while/body/eval_jaxpr/kcb,kce->cbe/dot_general | solution.py:53
  465.5 2.3 fusion.78
  469.7 2.1 add_bitcast_fusion.2
  479.2 2.9 constant_dynamic-slice_fusion.4
  482.1 3.4 copy.128
  488.0 8.6 %select_add_fusion.2 = f32[26,128,128]{2,1,0:T(8,128)} fusion(f32[26,128,128]{2,1,0:T(8,128)} %get-tuple-element.298, bf16[512,26,128]{2,1,0:T(8,128)(2,1)S(1)} %convert_bitcast_fusion.4, bf16[512,26,128]{2,1,0:T(8,128)(2,1)S(1)} %convert_bitcast_fusion.5, pred[]{:T(512)S(6)} %compare.7), kind=kOutput, calls=%fused_computation.17.clone.1 | convolution fusion | flops 437059584 | bytes 10223617 | tf_op jit(solution)/shard_map/while/body/eval_jaxpr/kcb,kce->cbe/dot_general | solution.py:53
  496.7 2.3 fusion.78
  500.9 2.1 add_bitcast_fusion.2
  510.4 2.9 constant_dynamic-slice_fusion.4
  513.3 3.4 copy.128
  519.3 8.6 %select_add_fusion.2 = f32[26,128,128]{2,1,0:T(8,128)} fusion(f32[26,128,128]{2,1,0:T(8,128)} %get-tuple-element.298, bf16[512,26,128]{2,1,0:T(8,128)(2,1)S(1)} %convert_bitcast_fusion.4, bf16[512,26,128]{2,1,0:T(8,128)(2,1)S(1)} %convert_bitcast_fusion.5, pred[]{:T(512)S(6)} %compare.7), kind=kOutput, calls=%fused_computation.17.clone.1 | convolution fusion | flops 437059584 | bytes 10223617 | tf_op jit(solution)/shard_map/while/body/eval_jaxpr/kcb,kce->cbe/dot_general | solution.py:53
  527.9 2.3 fusion.78
  532.1 2.1 add_bitcast_fusion.2
  541.7 2.9 constant_dynamic-slice_fusion.4
  544.5 3.4 copy.128
  550.5 8.6 %select_add_fusion.2 = f32[26,128,128]{2,1,0:T(8,128)} fusion(f32[26,128,128]{2,1,0:T(8,128)} %get-tuple-element.298, bf16[512,26,128]{2,1,0:T(8,128)(2,1)S(1)} %convert_bitcast_fusion.4, bf16[512,26,128]{2,1,0:T(8,128)(2,1)S(1)} %convert_bitcast_fusion.5, pred[]{:T(512)S(6)} %compare.7), kind=kOutput, calls=%fused_computation.17.clone.1 | convolution fusion | flops 437059584 | bytes 10223617 | tf_op jit(solution)/shard_map/while/body/eval_jaxpr/kcb,kce->cbe/dot_general | solution.py:53
  559.1 2.3 fusion.78
  572.9 2.9 constant_dynamic-slice_fusion.4
  575.8 3.4 copy.128
  581.7 8.6 %select_add_fusion.2 = f32[26,128,128]{2,1,0:T(8,128)} fusion(f32[26,128,128]{2,1,0:T(8,128)} %get-tuple-element.298, bf16[512,26,128]{2,1,0:T(8,128)(2,1)S(1)} %convert_bitcast_fusion.4, bf16[512,26,128]{2,1,0:T(8,128)(2,1)S(1)} %convert_bitcast_fusion.5, pred[]{:T(512)S(6)} %compare.7), kind=kOutput, calls=%fused_computation.17.clone.1 | convolution fusion | flops 437059584 | bytes 10223617 | tf_op jit(solution)/shard_map/while/body/eval_jaxpr/kcb,kce->cbe/dot_general | solution.py:53
  590.4 2.3 fusion.78
  604.1 2.9 constant_dynamic-slice_fusion.4
  607.0 3.4 copy.128
  612.9 8.6 %select_add_fusion.2 = f32[26,128,128]{2,1,0:T(8,128)} fusion(f32[26,128,128]{2,1,0:T(8,128)} %get-tuple-element.298, bf16[512,26,128]{2,1,0:T(8,128)(2,1)S(1)} %convert_bitcast_fusion.4, bf16[512,26,128]{2,1,0:T(8,128)(2,1)S(1)} %convert_bitcast_fusion.5, pred[]{:T(512)S(6)} %compare.7), kind=kOutput, calls=%fused_computation.17.clone.1 | convolution fusion | flops 437059584 | bytes 10223617 | tf_op jit(solution)/shard_map/while/body/eval_jaxpr/kcb,kce->cbe/dot_general | solution.py:53
  621.6 2.3 fusion.78
  635.6 6.9 fusion.38
  642.5 3.4 copy.111
  645.9 118.4 %reduce-scatter.2.cloned.1.call-done = f32[256,896]{1,0:T(8,128)} async-done(((f32[4096,896]{1,0:T(8,128)}), f32[256,896]{1,0:T(8,128)}) %reduce-scatter.2.cloned.1.call-update) | async-done | bytes 917520 | tf_op jit(solution)/shard_map/reduce_scatter | solution.py:93
  (118 shorter events, 113.4 us)
Async XLA Ops:
  7.2 81.7 %all-gather.3.cloned.1.call-start = ((), (), s32[]{:S(2)}) async-start(), calls=%async_computation.2 | async-start | bytes 7798784 | tf_op jit(solution)/shard_map/all_gather | solution.py:74
  8.3 19.2 %copy-start.2 = (s32[7,14]{1,0:T(8,128)S(1)}, s32[7,14]{1,0:T(8,128)}, u32[]{:S(2)}) copy-start(s32[7,14]{1,0:T(8,128)} %param.9) | copy-start | bytes 1180
  8.3 22.2 %copy-start.1 = (bf16[896,1792]{1,0:T(8,128)(2,1)S(1)}, bf16[896,1792]{1,0:T(8,128)(2,1)}, u32[]{:S(2)}) copy-start(bf16[896,1792]{1,0:T(8,128)(2,1)} %param.8) | copy-start | bytes 9633796
  23.5 354.6 %all-gather.5.cloned.1.call-start = ((), (), s32[]{:S(2)}) async-start(), calls=%async_computation.3 | async-start | bytes 16515072 | tf_op jit(solution)/shard_map/all_gather | solution.py:78
  27.4 736.9 %reduce-scatter.2.cloned.1.call-start = ((), (), s32[]{:S(2)}) async-start(), calls=%async_computation.4 | async-start | bytes 15597568 | tf_op jit(solution)/shard_map/reduce_scatter | solution.py:93
  396.0 7.1 copy-start
  425.7 8.6 %copy-start = (bf16[26,128,128]{2,1,0:T(8,128)(2,1)S(1)}, bf16[26,128,128]{2,1,0:T(8,128)(2,1)}, u32[]{:S(2)}) copy-start(bf16[26,128,128]{2,1,0:T(8,128)(2,1)} %get-tuple-element.314) | copy-start | bytes 2555908 | tf_op jit(solution)/shard_map/while
  456.9 8.6 %copy-start = (bf16[26,128,128]{2,1,0:T(8,128)(2,1)S(1)}, bf16[26,128,128]{2,1,0:T(8,128)(2,1)}, u32[]{:S(2)}) copy-start(bf16[26,128,128]{2,1,0:T(8,128)(2,1)} %get-tuple-element.314) | copy-start | bytes 2555908 | tf_op jit(solution)/shard_map/while
  488.0 8.6 %copy-start = (bf16[26,128,128]{2,1,0:T(8,128)(2,1)S(1)}, bf16[26,128,128]{2,1,0:T(8,128)(2,1)}, u32[]{:S(2)}) copy-start(bf16[26,128,128]{2,1,0:T(8,128)(2,1)} %get-tuple-element.314) | copy-start | bytes 2555908 | tf_op jit(solution)/shard_map/while
  519.3 8.6 %copy-start = (bf16[26,128,128]{2,1,0:T(8,128)(2,1)S(1)}, bf16[26,128,128]{2,1,0:T(8,128)(2,1)}, u32[]{:S(2)}) copy-start(bf16[26,128,128]{2,1,0:T(8,128)(2,1)} %get-tuple-element.314) | copy-start | bytes 2555908 | tf_op jit(solution)/shard_map/while
  550.5 8.6 %copy-start = (bf16[26,128,128]{2,1,0:T(8,128)(2,1)S(1)}, bf16[26,128,128]{2,1,0:T(8,128)(2,1)}, u32[]{:S(2)}) copy-start(bf16[26,128,128]{2,1,0:T(8,128)(2,1)} %get-tuple-element.314) | copy-start | bytes 2555908 | tf_op jit(solution)/shard_map/while
  581.7 8.6 %copy-start = (bf16[26,128,128]{2,1,0:T(8,128)(2,1)S(1)}, bf16[26,128,128]{2,1,0:T(8,128)(2,1)}, u32[]{:S(2)}) copy-start(bf16[26,128,128]{2,1,0:T(8,128)(2,1)} %get-tuple-element.314) | copy-start | bytes 2555908 | tf_op jit(solution)/shard_map/while
  612.9 8.6 %copy-start = (bf16[26,128,128]{2,1,0:T(8,128)(2,1)S(1)}, bf16[26,128,128]{2,1,0:T(8,128)(2,1)}, u32[]{:S(2)}) copy-start(bf16[26,128,128]{2,1,0:T(8,128)(2,1)} %get-tuple-element.314) | copy-start | bytes 2555908 | tf_op jit(solution)/shard_map/while
Sparse Core Ops, SparseCore 0:
  23.6 65.1 all-gather.2
  91.1 286.9 all-gather.4
  633.0 131.2 reduce-scatter.1
where the time goes:
time: 786 us; the launch traced here: 773 us
  waiting for transfers between devices  441 us (56%)
  matrix products  165 us (21%)
  local copies, waits for them, and re-layouts  129 us (16%)
  blocking collectives  15.2 us (2%)
  between operations  14 us (2%)
    all_gather x1, waiting for transfers between devices, on_device(): piece = lax.all_gather(grad_out, 'col', axis=0, tiled=True)  289 us
    reduce_scatter x1, waiting for transfers between devices, on_device(): lax.psum_scatter(input_sum, 'row', scatter_dimension=0, tiled=True)  118 us
    dot_general x8, matrix products, weight_term(): jnp.einsum('kcb,kce->cbe', xsel, chosen, preferred_element_type=jnp.float32)  67.5 us
    all_gather x1, waiting for transfers between devices, on_device(): x_full = lax.all_gather(x_local, 'row', axis=0, tiled=True)  33.4 us
    reshape x8, local copies, waits for them, and re-layouts, select_grads(): grows.reshape(rows, fblk, blk)  27 us
    dynamic_update_slice x16, local copies, waits for them, and re-layouts, step(): lax.dynamic_update_slice_in_dim(xsum, input_term(grows, chosen), offset, 0)  25.5 us
    dynamic_slice x8, local copies, waits for them, and re-layouts, step(): grows = lax.dynamic_slice_in_dim(piece, offset, sub, 0)  22.8 us
    dot_general x8, matrix products, input_term(): jnp.einsum('kce,cbe->kcb', chosen, live_w, preferred_element_type=jnp.flo...  18.1 us
  transfers between devices with their start and end apart: 3, of which 3 were waited for; matrix products, arithmetic and copies ran while one was open for 6% of the time, Pallas kernels for 0%

commit v1 on v0

v1 whole, which is shorter than its diff:
```python
import functools
import itertools

import jax
import jax.numpy as jnp
import numpy as np
from jax import lax
from jax.experimental import pallas as pl
from jax.experimental.pallas import tpu as pltpu
from jax.sharding import Mesh, PartitionSpec as P

AXES = ("y", "xh", "co", "z", "xl")
SIZES = (4, 2, 2, 4, 2)
BLK = 128
CAP = 26
ROWS = 32
PARTS = 2
F32 = jnp.float32
BF16 = jnp.bfloat16
COORDS = list(itertools.product(*(range(n) for n in SIZES)))
VMEM = pl.BlockSpec(memory_space=pltpu.VMEM)
SMEM = pl.BlockSpec(memory_space=pltpu.SMEM)
ANY = pl.BlockSpec(memory_space=pl.ANY)
Y, XH, CO, Z, XL = range(5)


def send(value, target):
    pairs = []
    for at in COORDS:
        to = target(*at)
        if to is not None:
            pairs.append((COORDS.index(at), COORDS.index(to)))
    return lax.ppermute(value, AXES, pairs)


def to_y(step):
    return lambda y, xh, co, z, xl: ((y + step) % 4, xh, co, z, xl)


def to_z(step):
    return lambda y, xh, co, z, xl: (y, xh, co, (z + step) % 4, xl)


def to_core(y, xh, co, z, xl):
    return (y, xh, 1 - co, z, xl)


def to_pair(y, xh, co, z, xl):
    return (y, xh, co, z, 1 - xl)


def along_x(moves):
    def target(y, xh, co, z, xl):
        x = 2 * xh + xl
        if x not in moves:
            return None
        return (y, moves[x] // 2, co, z, moves[x] % 2)

    return target


def out(shape, dtype=BF16):
    return jax.ShapeDtypeStruct(shape, dtype)


def call(kernel, ins, outs, operands, scratch=(), flops=0, limit=28):
    return pl.pallas_call(
        kernel,
        out_shape=tuple(shape for shape, _ in outs),
        in_specs=list(ins),
        out_specs=tuple(spec for _, spec in outs),
        scratch_shapes=list(scratch),
        compiler_params=pltpu.CompilerParams(vmem_limit_bytes=limit * 2 ** 20),
        cost_estimate=pl.CostEstimate(flops=flops, bytes_accessed=max(1024, flops // 200), transcendentals=0),
    )(*operands)


def move(pairs, sems):
    copies = [
        pltpu.make_async_copy(source, target, sems.at[n])
        for n, (source, target) in enumerate(pairs)
    ]
    for copy in copies:
        copy.start()
    return copies


def list_live(mask_ref, list_ref):
    dblk, fblk = mask_ref.shape
    for slot in range(CAP):
        list_ref[slot] = fblk

    def row(i, slot):
        list_ref[ROWS + i] = slot

        def one(j, slot):
            is_live = mask_ref[i, j]

            @pl.when(is_live == 1)
            def _():
                list_ref[slot] = i * 16 + j

            return slot + is_live

        return lax.fori_loop(0, fblk, one, slot)

    list_ref[ROWS + dblk] = lax.fori_loop(0, dblk, row, jnp.int32(0))


def stacked(sources, target):
    pairs, start = [], 0
    for source in sources:
        size = source.shape[0]
        pairs.append((source, target.at[pl.ds(start, size)]))
        start += size
    return pairs


def each_slot(list_ref, body):
    def one(slot, _):
        place = list_ref[slot]
        body(place >> 4, place & 15, slot)
        return 0

    lax.fori_loop(0, CAP, one, 0)


def span(index):
    return pl.ds(pl.multiple_of(index * BLK, BLK), BLK)


def slices_kernel(at_ref, x_ref, x0, x1, x2, x3, sems):
    z, xh = at_ref[Z], at_ref[XH]
    depth = x0.shape[1] // 2
    pairs = []
    for step, x_out in enumerate((x0, x1, x2, x3)):
        there = (z + step) % 4
        for tile, which in enumerate((xh, 1 - xh)):
            start = pl.multiple_of((there * 2 + which) * depth, BLK)
            pairs.append(
                (x_ref.at[:, pl.ds(start, depth)], x_out.at[:, pl.ds(tile * depth, depth)])
            )
    for copy in move(pairs, sems):
        copy.wait()


def compact_kernel(mask_ref, w_ref, out_ref, list_ref, held, sems):
    list_live(mask_ref, list_ref)
    last = mask_ref.shape[1] - 1
    copies = []
    for slot in range(CAP):
        place = list_ref[slot]
        source = w_ref.at[span(place >> 4), span(jnp.minimum(place & 15, last))]
        copies.append(pltpu.make_async_copy(source, held.at[slot], sems.at[slot]))
        copies[slot].start()
    for slot in range(CAP):
        copies[slot].wait()
        out_ref[slot] = held[slot].T


def order_kernel(at_ref, x0, x1, x2, x3, out_ref, sems):
    z = at_ref[Z]
    pairs = [(x_in, out_ref.at[(z + step) % 4]) for step, x_in in enumerate((x0, x1, x2, x3))]
    for copy in move(pairs, sems):
        copy.wait()


def turn_kernel(at_ref, mine, got_a, got_b, out_ref, rows):
    x = at_ref[XH] * 2 + at_ref[XL]
    count = mine.shape[1]

    def put(source, which):
        for n in range(4):
            rows[(2 * n + which) * count : (2 * n + which + 1) * count, :] = source[n]

    for which, near, far in ((0, 0, 1), (1, 3, 2)):
        pl.when(x == near)(functools.partial(put, mine, which))
        pl.when(x == far)(functools.partial(put, got_b, which))
        pl.when((x != near) & (x != far))(functools.partial(put, got_a, which))
    tiles, depth, _ = out_ref.shape
    for tile in range(tiles):
        for i in range(depth // BLK):
            start = tile * depth + i * BLK
            out_ref[tile, i * BLK : (i + 1) * BLK, :] = rows[:, start : start + BLK].T


def partial_kernel(count, at_ref, list_ref, pair_list_ref, blocks_ref, pair_blocks_ref, *refs):
    co = at_ref[CO]
    g_refs, refs = refs[:-9], refs[-9:]
    keep_ref, give_ref, blocks, grows, total, sums, g_sems, w_sems, o_sems = refs
    toks, depth = sums.shape[2], sums.shape[3] // 2
    loads = move(stacked(g_refs, grows), g_sems)
    loads += move([(blocks_ref, blocks.at[0]), (pair_blocks_ref, blocks.at[1])], w_sems)
    for load in loads:
        load.wait()

    def rows_of(place):
        return grows[:, span(place & 15)]

    stores = []
    for tile, slots in enumerate((list_ref, pair_list_ref)):

        def row(i, _):
            first, end = slots[ROWS + i], slots[ROWS + i + 1]
            total[...] = jnp.zeros_like(total)

            def add(slot, size):
                left = [rows_of(slots[slot + n]) for n in range(size)]
                right = blocks[tile, pl.ds(slot, size)].reshape(size * BLK, BLK)
                total[...] += jnp.dot(
                    jnp.concatenate(left, axis=1), right, preferred_element_type=F32
                )

            def four(n, _):
                add(first + 4 * n, 4)
                return 0

            size = end - first
            lax.fori_loop(0, size >> 2, four, 0)
            pl.when((size & 2) == 2)(lambda: add(first + ((size >> 2) << 2), 2))
            pl.when((size & 1) == 1)(lambda: add(end - 1, 1))
            cols = span(i + tile * (depth // BLK))
            for r in range(2 * count):
                rows = total[r * toks : (r + 1) * toks, :].astype(BF16)
                sums[(r % 2) ^ co, r // 2, :, cols] = rows
            return 0

        lax.fori_loop(0, depth // BLK, row, 0)
        half = pl.ds(tile * depth, depth)
        stores += move(
            [
                (sums.at[1, :, :, half], give_ref.at[:, :, half]),
                (sums.at[0, :, :, half], keep_ref.at[:, :, half]),
            ],
            o_sems.at[pl.ds(2 * tile, 2)],
        )
    for store in stores:
        store.wait()


def add_core_kernel(at_ref, near, far, near_got, far_got, *outs):
    toks = outs[0].shape[0]
    half = toks // 2
    chunks = ((near, near_got, 0), (near, near_got, 1), (far, far_got, 0), (near, near_got, 2))

    def cut(turn):
        def total(step, start, size):
            kept, got, n = chunks[(step + turn) % 4]
            rows = pl.ds(start, size)
            return (kept[n, rows, :].astype(F32) + got[n, rows, :].astype(F32)).astype(BF16)

        low, high = outs[-2:]
        for part in range(PARTS):
            base, up, down = outs[3 * part : 3 * part + 3]
            start = part * toks
            base[...] = total(0, start, toks)
            up[...] = total(1, start, toks)
            down[...] = total(3, start, toks)
            low[part] = total(2, start, half)
            high[part] = total(2, start + half, half)

    turned = (at_ref[Y] - at_ref[Z]) & 3
    for turn in range(4):
        pl.when(turned == turn)(functools.partial(cut, turn))


def add_far_kernel(part, up, down, low, high, up_out, down_out):
    half = low.shape[1]
    up_out[:half] = (up[:half].astype(F32) + low[part].astype(F32)).astype(BF16)
    up_out[half:] = up[half:]
    down_out[:half] = down[:half]
    down_out[half:] = (down[half:].astype(F32) + high[part].astype(F32)).astype(BF16)


def add_near_kernel(at_ref, base, up, down, own, to_a, to_b):
    xh, xl = at_ref[XH], at_ref[XL]
    total = base[...].astype(F32) + up[...].astype(F32) + down[...].astype(F32)
    total = total.astype(BF16)
    depth = own.shape[1]
    first, second = total[:, :depth], total[:, depth:]
    own[...] = first

    def put(to_first, to_second):
        to_first[...] = first
        to_second[...] = second

    pl.when(xh == xl)(functools.partial(put, to_b, to_a))
    pl.when(xh != xl)(functools.partial(put, to_a, to_b))


def add_last_kernel(at_ref, own0, a0, b0, own1, a1, b1, out_ref):
    x = at_ref[XH] * 2 + at_ref[XL]
    half = own0.shape[0]

    def put(rows, one, two):
        out_ref[rows, :] = (one[...].astype(F32) + two[...].astype(F32)).astype(BF16)

    for part, (own, a, b) in enumerate(((own0, a0, b0), (own1, a1, b1))):
        rows = pl.ds(part * half, half)
        at_end = (x == 0) | (x == 3)
        pl.when(at_end)(functools.partial(put, rows, a, own))
        pl.when(jnp.logical_not(at_end))(functools.partial(put, rows, a, b))


def weight_kernel(tile, chunks, adds, at_ref, list_ref, *refs):
    y, z, co = at_ref[Y], at_ref[Z], at_ref[CO]
    x_refs, refs = refs[:10], refs[10:]
    g_refs, (out_ref, turned, grows, x_sems, g_sems) = refs[:-5], refs[-5:]
    if adds:
        terms, g_refs = g_refs[-1], g_refs[:-1]
    hidden = grows.shape[1]
    toks = x_refs[0].shape[2]
    g_loads = move(stacked(g_refs, grows), g_sems)
    x_loads = []
    for core, (mine, above, below, *far) in ((co, x_refs[:5]), (1 - co, x_refs[5:])):
        for step, source in enumerate((mine.at[tile], above.at[tile], far[tile], below.at[tile])):
            step = (y + step - z) & 3
            needed, spot = step >= 0, step
            if len(chunks) == 3:
                needed, spot = step != 2, step - (step >> 1)
            elif len(chunks) == 2:
                needed, spot = (step >> 1) == (chunks[0] >> 1), step & 1
            lanes = pl.ds(pl.multiple_of((spot * 2 + core) * toks, BLK), toks)
            load = pltpu.make_async_copy(source, turned.at[:, lanes], x_sems.at[len(x_loads)])
            pl.when(needed)(load.start)
            x_loads.append((needed, load))
    for needed, load in x_loads:
        pl.when(needed)(load.wait)
    for load in g_loads:
        load.wait()
    last = hidden // BLK - 1
    for slot in range(CAP):
        place = list_ref[slot]
        i, j = place >> 4, jnp.minimum(place & 15, last)
        total = jnp.dot(
            turned[span(i), :],
            grows[:, span(j)],
            preferred_element_type=F32,
        )
        if adds:
            total = total + terms[slot]
        out_ref[slot] = total.astype(out_ref.dtype)


def combine_kernel(list_ref, own_ref, got_ref, out_ref):
    out_ref[...] = jnp.zeros_like(out_ref)
    last = out_ref.shape[1] // BLK - 1

    def body(i, j, slot):
        @pl.when(j <= last)
        def _():
            out_ref[span(i), span(j)] = (own_ref[slot] + got_ref[slot].astype(F32)).astype(BF16)

    each_slot(list_ref, body)


def after(value, *others):
    return lax.optimization_barrier((value, others))[0]


def on_device(x_act, grad_out, weight, block_mask):
    place = jnp.stack([lax.axis_index(name) for name in AXES]).astype(jnp.int32)
    depth, hidden = weight.shape
    wide = 2 * depth
    chunk = grad_out.shape[0] // 2
    toks = chunk // PARTS
    few = x_act.shape[0]
    dma = pltpu.SemaphoreType.DMA

    def blocks_of(dtype):
        return (out((CAP, BLK, BLK), dtype), VMEM)

    pair_mask = send(block_mask, to_pair)
    x0, x1, x2, x3 = call(
        slices_kernel, [SMEM, VMEM], [(out((few, wide)), ANY)] * 4,
        (place, x_act), [dma((8,))],
    )
    x_from1 = send(x3, to_z(3))
    x_from2 = send(x2, to_z(2))
    x_from3 = send(x1, to_z(1))

    mine = after(grad_out, x_from1, x_from2, x_from3, pair_mask)
    below = send(mine, to_z(1))
    above = send(mine, to_z(-1))

    (by_z,) = call(
        order_kernel, [SMEM] + [ANY] * 4, [(out((4, few, wide)), ANY)],
        (place, after(x0, pair_mask), x_from1, x_from2, x_from3), [dma((4,))],
    )
    slot_list = (out((ROWS + 8,), jnp.int32), SMEM)
    blocks, slots = call(
        compact_kernel, [SMEM, ANY], [blocks_of(BF16), slot_list],
        (after(block_mask, by_z), weight),
        [pltpu.VMEM((CAP, BLK, BLK), BF16), dma((CAP,))], limit=28,
    )
    pair_blocks = send(blocks, to_pair)
    got_a = send(by_z, along_x({0: 2, 1: 0, 2: 3, 3: 1}))
    got_b = send(by_z, along_x({1: 2, 2: 1}))
    (turned,) = call(
        turn_kernel, [SMEM] + [VMEM] * 3, [(out((2, depth, 8 * few)), VMEM)],
        (place, after(by_z, blocks), got_a, got_b), [pltpu.VMEM((8 * few, wide), BF16)], flops=10 ** 10,
    )
    x_below = send(turned, to_y(1))
    x_above = send(turned, to_y(-1))

    def partials(*grads, flops=0):
        count = sum(grad.shape[0] for grad in grads) // (2 * chunk)
        return call(
            functools.partial(partial_kernel, count), [SMEM] * 3 + [ANY] * (2 + len(grads)),
            [(out((count, chunk, wide)), ANY)] * 2,
            (place, slots, pair_slots, blocks, pair_blocks) + grads,
            [
                pltpu.VMEM((2, CAP, BLK, BLK), BF16),
                pltpu.VMEM((2 * count * chunk, hidden), BF16),
                pltpu.VMEM((2 * count * chunk, BLK), F32),
                pltpu.VMEM((2, count, chunk, wide), BF16),
                dma((len(grads),)), dma((2,)), dma((4,)),
            ],
            flops=flops,
        )

    (pair_slots,) = call(
        list_live, [SMEM], [slot_list], (after(pair_mask, pair_blocks),), flops=5 * 10 ** 9
    )
    far_low, far_high = below[:chunk], above[chunk:]
    far_slices = (far_low, far_high)
    far_low = send(far_low, to_z(1))
    far_high = send(far_high, to_z(-1))
    x_near = tuple(send(value, to_core) for value in (after(turned, pair_slots), x_above, x_below))
    x_low, x_high = after((x_below[0], x_above[1]), far_slices, x_near)
    x_low = send(x_low, to_y(1))
    x_high = send(x_high, to_y(-1))
    near, near_give = partials(
        *after((grad_out, above, below), far_slices, x_near), flops=10 ** 10
    )
    near_got = send(after(near_give, far_low, far_high, x_low, x_high), to_core)
    far, far_give = partials(*after((far_low, far_high), near, x_near))
    far_got = send(far_give, to_core)

    every = (
        (0, (grad_out,)), (1, (above,)), (2, (far_low, far_high)), (3, (below,)),
    )

    def weight_grad(tile, dtype, chunks, terms=(), flops=0, last=()):
        grads = sum((values for chunk_at, values in every if chunk_at in chunks), ())
        (sums,) = call(
            functools.partial(weight_kernel, tile, chunks, bool(terms)),
            [SMEM] * 2 + [ANY] * (10 + len(grads)) + [VMEM] * len(terms), [blocks_of(dtype)],
            (after(place, last), (slots, pair_slots)[tile]) + inputs + grads + terms,
            [
                pltpu.VMEM((depth, 2 * len(chunks) * chunk), BF16),
                pltpu.VMEM((2 * len(chunks) * chunk, hidden), BF16),
                dma((8,)), dma((len(grads),)),
            ],
            flops=flops,
        )
        return sums

    row = (out((toks, wide)), VMEM)
    half_rows = (out((PARTS, toks // 2, wide)), VMEM)
    cuts = call(
        add_core_kernel, [SMEM] + [VMEM] * 4, [row] * 3 * PARTS + [half_rows] * 2,
        (place, near, far, near_got, far_got),
    )
    low, high = send(cuts[-2], to_y(1)), send(cuts[-1], to_y(-1))
    x_far = tuple(send(after(value, far), to_core) for value in (x_low, x_high))
    inputs = (turned, x_above, x_below, x_low, x_high) + x_near + x_far
    pair_sum = weight_grad(1, BF16, (0, 1, 2, 3), (), 2 * 10 ** 10, cuts[0])
    pair_got = send(pair_sum, to_pair)
    ends = []
    last = pair_sum
    for part in range(PARTS):
        base, up, down = cuts[3 * part : 3 * part + 3]
        up, down = call(
            functools.partial(add_far_kernel, part), [VMEM] * 4, [row] * 2,
            after((up, down), last) + (low, high),
        )
        ends.append((base, send(up, to_y(1)), send(down, to_y(-1))))
        last = up
    last = own_sum = weight_grad(0, F32, (0, 1, 2, 3), (), 0, last)
    parts = ()
    for base, up, down in ends:
        mine, to_a, to_b = call(
            add_near_kernel, [SMEM] + [VMEM] * 3, [(out((toks, depth)), VMEM)] * 3,
            (place, after(base, last), up, down),
        )
        got_a = send(to_a, along_x({0: 1, 2: 0, 1: 3, 3: 2}))
        got_b = send(to_b, along_x({2: 1, 1: 2}))
        parts += (mine, got_a, got_b)
        last = (got_a, got_b)

    (grad_weight,) = call(
        combine_kernel, [SMEM, VMEM, VMEM], [(out(weight.shape), VMEM)], (slots, own_sum, pair_got),
        flops=10 ** 10,
    )
    (grad_in,) = call(
        add_last_kernel, [SMEM] + [VMEM] * 6, [(out((chunk, depth)), VMEM)], (place,) + parts
    )
    return grad_in, grad_weight


def solution(mesh):
    fine = Mesh(np.asarray(mesh.devices).reshape(SIZES), AXES)
    rows, cols = AXES[:3], AXES[3:]
    return jax.shard_map(
        on_device,
        mesh=fine,
        in_specs=(P(AXES, None), P(cols, rows), P(cols, rows), P(cols, rows)),
        out_specs=(P(rows, cols), P(cols, rows)),
        check_vma=False,
    )
```

time: 786 us -> 151 us (0.19); the launches traced: 773 us -> 150 us
  waiting for transfers between devices: 441 us -> 62.4 us
  matrix products: 165 us -> 0 us
  local copies, waits for them, and re-layouts: 129 us -> 3.89 us
  Pallas kernels: 0 us -> 45 us
  starting transfers between devices: 0.12 us -> 38.3 us
  blocking collectives: 15.2 us -> 0 us
  between operations: 14 us -> 0.91 us
    all_gather x2 -> x0, waiting for transfers between devices: 323 us -> none  [the longest x1 289 us: on_device(): piece = lax.all_gather(grad_out, 'col', axis=0, tiled=True)]
    dot_general x51 -> x0, matrix products: 165 us -> none  [the longest x8 67.5 us: weight_term(): jnp.einsum('kcb,kce->cbe', xsel, chosen, preferred_element_type=jnp.float32)]
    reduce_scatter x1 -> x0, waiting for transfers between devices: 118 us -> none  [on_device(): lax.psum_scatter(input_sum, 'row', scatter_dimension=0, tiled=True)]
    ppermute x0 -> x33, waiting for transfers between devices: none -> 62.4 us  [send(): return lax.ppermute(value, AXES, pairs)]
    pallas_call x0 -> x16, Pallas kernels: none -> 45 us  [call(): pl.pallas_call(kernel, out_shape=tuple((shape for shape, _ in outs)), in_...]
    ppermute x0 -> x33, starting transfers between devices: none -> 38.3 us  [send(): return lax.ppermute(value, AXES, pairs)]
    dynamic_slice x24 -> x0, local copies, waits for them, and re-layouts: 37.1 us -> none  [the longest x8 22.8 us: step(): grows = lax.dynamic_slice_in_dim(piece, offset, sub, 0)]
    reshape x18 -> x0, local copies, waits for them, and re-layouts: 36.9 us -> none  [the longest x8 27 us: select_grads(): grows.reshape(rows, fblk, blk)]
  transfers between devices with their start and end apart: 3 -> 33, of which waited for: 3 -> 15; matrix products, arithmetic and copies ran while one was open for 6% -> 0% of each run, Pallas kernels for 0% -> 28%
where the time goes in v1:
time: 151 us; the launch traced here: 150 us
  waiting for transfers between devices  62.4 us (41%)
  Pallas kernels  45 us (30%)
  starting transfers between devices  38.3 us (25%)
  local copies, waits for them, and re-layouts  3.89 us (3%)
    ppermute x33, waiting for transfers between devices, send(): return lax.ppermute(value, AXES, pairs)  62.4 us
    pallas_call x16, Pallas kernels, call(): pl.pallas_call(kernel, out_shape=tuple((shape for shape, _ in outs)), in_...  45 us
    ppermute x33, starting transfers between devices, send(): return lax.ppermute(value, AXES, pairs)  38.3 us
    unnamed x8, local copies, waits for them, and re-layouts  3.62 us
  transfers between devices with their start and end apart: 33, of which 15 were waited for; matrix products, arithmetic and copies ran while one was open for 0% of the time, Pallas kernels for 28%

profile of v1, /device:TPU:26, one launch (start us, length us, event | category | flops | bytes accessed | tf_op | source)
XLA Modules:
  0.0 150.4 jit_solution(13801523074779932816)
XLA Ops:
  0.7 1.0 copy-done.2
  1.7 0.8 shard_map.59
  2.5 4.1 %collective-permute-start.1 = (bf16[32,1792]{1,0:T(8,128)(2,1)S(1)}, bf16[32,1792]{1,0:T(8,128)(2,1)S(1)}, u32[]{:S(2)}, u32[]{:S(2)}) collective-permute-start(bf16[32,1792]{1,0:T(8,128)(2,1)S(1)} %get-tuple-element.56), channel_id=1, source_target_pairs={{0,6},{1,7},{2,0},{3,1},{4,2},{5,3},{6,4},{7,5},{8,14},{9,15},{10,... | collective-permute-start | bytes 344072 | tf_op jit(solution)/shard_map/ppermute | solution.py:33
  6.6 1.3 collective-permute-start.3
  8.4 3.3 %collective-permute-done.mask_ref = s32[7,14]{1,0:T(8,128)S(1)} collective-permute-done((s32[7,14]{1,0:T(8,128)}, s32[7,14]{1,0:T(8,128)S(1)}, u32[]{:S(2)}, u32[]{:S(2)}) %collective-permute-start) | collective-permute-done | bytes 424 | tf_op jit(solution)/shard_map/ppermute | solution.py:33
  11.7 2.3 %collective-permute-done.2.x2 = bf16[32,1792]{1,0:T(8,128)(2,1)S(1)} collective-permute-done((bf16[32,1792]{1,0:T(8,128)(2,1)S(1)}, bf16[32,1792]{1,0:T(8,128)(2,1)S(1)}, u32[]{:S(2)}, u32[]{:S(2)}) %collective-permute-start.2) | collective-permute-done | bytes 114720 | tf_op jit(solution)/shard_map/ppermute | solution.py:33
  14.0 0.9 collective-permute-done.3.x3
  14.9 1.2 shard_map.60.mine
  16.1 0.6 collective-permute-start.7
  16.7 4.0 %collective-permute-start.8 = (bf16[4,32,1792]{2,1,0:T(8,128)(2,1)S(1)}, bf16[4,32,1792]{2,1,0:T(8,128)(2,1)S(1)}, u32[]{:S(2)}, u32[]{:S(2)}) collective-permute-start(bf16[4,32,1792]{2,1,0:T(8,128)(2,1)S(1)} %shard_map.60.mine), channel_id=1, source_target_pairs={{1,16},{3,18},{5,20},{7,22},{9,24},{11,26},{13,28},{15,30},{16,1},... | collective-permute-start | bytes 1376264 | tf_op jit(solution)/shard_map/ppermute | solution.py:33
  20.8 1.0 collective-permute-start.5
  21.7 1.1 collective-permute-start.6
  22.9 1.9 %copy-done = bf16[896,1792]{1,0:T(8,128)(2,1)S(1)} copy-done((bf16[896,1792]{1,0:T(8,128)(2,1)S(1)}, bf16[896,1792]{1,0:T(8,128)(2,1)}, u32[]{:S(2)}) %copy-start) | copy-done | bytes 3211288
  24.8 0.7 copy-done.3
  25.5 4.4 %shard_map.61 = (bf16[26,128,128]{2,1,0:T(8,128)(2,1)S(1)}, s32[40]{0:T(128)S(1)}) custom-call(s32[7,14]{1,0:T(8,128)S(1)} %copy-done.3, bf16[896,1792]{1,0:T(8,128)(2,1)S(1)} %copy-done), custom_call_target="tpu_custom_call" | custom-call | bytes 1024 | tf_op jit(solution)/shard_map/pallas_call | solution.py:67
  30.0 9.6 %collective-permute-done.8.got_b = bf16[4,32,1792]{2,1,0:T(8,128)(2,1)S(1)} collective-permute-done((bf16[4,32,1792]{2,1,0:T(8,128)(2,1)S(1)}, bf16[4,32,1792]{2,1,0:T(8,128)(2,1)S(1)}, u32[]{:S(2)}, u32[]{:S(2)}) %collective-permute-start.8) | collective-permute-done | bytes 458784 | tf_op jit(solution)/shard_map/ppermute | solution.py:33
  39.6 0.9 shard_map.63.refs_0_
  40.5 0.8 collective-permute-start.10
  41.3 2.5 %collective-permute-start.12 = (bf16[2,896,256]{2,1,0:T(8,128)(2,1)S(1)}, bf16[2,896,256]{2,1,0:T(8,128)(2,1)S(1)}, u32[]{:S(2)}, u32[]{:S(2)}) collective-permute-start(bf16[2,896,256]{2,1,0:T(8,128)(2,1)S(1)} %shard_map.63.refs_0_), channel_id=1, source_target_pairs={{0,32},{1,33},{2,34},{3,35},{4,36},{5,37},{6,38},{7,39},{8,40},{9,... | collective-permute-start | bytes 2752520 | tf_op jit(solution)/shard_map/ppermute | solution.py:33
  43.8 5.5 %collective-permute-done.4.pair_blocks_ref = bf16[26,128,128]{2,1,0:T(8,128)(2,1)S(1)} collective-permute-done((bf16[26,128,128]{2,1,0:T(8,128)(2,1)S(1)}, bf16[26,128,128]{2,1,0:T(8,128)(2,1)S(1)}, u32[]{:S(2)}, u32[]{:S(2)}) %collective-permute-start.4) | collective-permute-done | bytes 852000 | tf_op jit(solution)/shard_map/ppermute | solution.py:33
  49.3 2.0 %shard_map.62.pair_list_ref.list_ref = s32[40]{0:T(128)S(1)} custom-call(s32[7,14]{1,0:T(8,128)S(1)} %collective-permute-done.mask_ref), custom_call_target="tpu_custom_call" | custom-call | flops 5000000000 | bytes 25000000 | tf_op jit(solution)/shard_map/pallas_call | solution.py:67
  51.5 12.6 %collective-permute-done.10.refs_1_ = bf16[2,896,256]{2,1,0:T(8,128)(2,1)S(1)} collective-permute-done((bf16[2,896,256]{2,1,0:T(8,128)(2,1)S(1)}, bf16[2,896,256]{2,1,0:T(8,128)(2,1)S(1)}, u32[]{:S(2)}, u32[]{:S(2)}) %collective-permute-start.10) | collective-permute-done | bytes 917536 | tf_op jit(solution)/shard_map/ppermute | solution.py:33
  64.9 3.3 %collective-permute-start.15 = (bf16[256,1792]{1,0:T(8,128)(2,1)S(1)}, bf16[256,1792]{1,0:T(8,128)(2,1)S(1)}, u32[]{:S(2)}, u32[]{:S(2)}) collective-permute-start(bf16[256,1792]{1,0:T(8,128)(2,1)S(1)} %slice.17), channel_id=1, source_target_pairs={{0,6},{1,7},{2,0},{3,1},{4,2},{5,3},{6,4},{7,5},{8,14},{9,15},{10,... | collective-permute-start | bytes 2752520 | tf_op jit(solution)/shard_map/ppermute | solution.py:33
  68.2 2.5 %collective-permute-start.16 = (bf16[896,256]{1,0:T(8,128)(2,1)S(1)}, bf16[896,256]{1,0:T(8,128)(2,1)S(1)}, u32[]{:S(2)}, u32[]{:S(2)}) collective-permute-start(bf16[896,256]{1,0:T(8,128)(2,1)S(1)} %slice_bitcast_fusion.1), channel_id=1, source_target_pairs={{0,32},{1,33},{2,34},{3,35},{4,36},{5,37},{6,38},{7,39},{8,40},{9,... | collective-permute-start | bytes 1376264 | tf_op jit(solution)/shard_map/ppermute | solution.py:33
  70.7 10.1 %shard_map.64 = (bf16[3,256,1792]{2,1,0:T(8,128)(2,1)S(1)}, bf16[3,256,1792]{2,1,0:T(8,128)(2,1)S(1)}) custom-call(s32[5]{0:T(128)S(1)} %stack.23.at_ref, s32[40]{0:T(128)S(1)} %get-tuple-element.60.list_ref, s32[40]{0:T(128)S(1)} %shard_map.62.pair_list_ref.list_ref, bf16[26,128,128]{2,1,0:T(8,128)(2,1)S(1)} %get-tuple-element.61.blocks_ref, ...), custom_call_target="tpu_custom_call" | custom-call | flops 10000000000 | bytes 50000000 | tf_op jit(solution)/shard_map/pallas_call | solution.py:67
  80.8 7.5 %collective-permute-done.14.refs_0_.refs_12_ = bf16[256,1792]{1,0:T(8,128)(2,1)S(1)} collective-permute-done((bf16[256,1792]{1,0:T(8,128)(2,1)S(1)}, bf16[256,1792]{1,0:T(8,128)(2,1)S(1)}, u32[]{:S(2)}, u32[]{:S(2)}) %collective-permute-start.14) | collective-permute-done | bytes 917536 | tf_op jit(solution)/shard_map/ppermute | solution.py:33
  88.4 6.3 %shard_map.65 = (bf16[1,256,1792]{2,1,0:T(8,128)(2,1)S(1)}, bf16[1,256,1792]{2,1,0:T(8,128)(2,1)S(1)}) custom-call(s32[5]{0:T(128)S(1)} %stack.23.at_ref, s32[40]{0:T(128)S(1)} %get-tuple-element.60.list_ref, s32[40]{0:T(128)S(1)} %shard_map.62.pair_list_ref.list_ref, bf16[26,128,128]{2,1,0:T(8,128)(2,1)S(1)} %get-tuple-element.61.blocks_ref, ...), custom_call_target="tpu_custom_call" | custom-call | bytes 1024 | tf_op jit(solution)/shard_map/pallas_call | solution.py:67
  94.7 0.9 collective-permute-start.19
  96.1 1.6 %collective-permute-done.19.far_got = bf16[1,256,1792]{2,1,0:T(8,128)(2,1)S(1)} collective-permute-done((bf16[1,256,1792]{2,1,0:T(8,128)(2,1)S(1)}, bf16[1,256,1792]{2,1,0:T(8,128)(2,1)S(1)}, u32[]{:S(2)}, u32[]{:S(2)}) %collective-permute-start.19) | collective-permute-done | bytes 917536 | tf_op jit(solution)/shard_map/ppermute | solution.py:33
  97.7 1.4 shard_map.66
  99.1 3.5 %collective-permute-start.22 = (bf16[2,64,1792]{2,1,0:T(8,128)(2,1)S(1)}, bf16[2,64,1792]{2,1,0:T(8,128)(2,1)S(1)}, u32[]{:S(2)}, u32[]{:S(2)}) collective-permute-start(bf16[2,64,1792]{2,1,0:T(8,128)(2,1)S(1)} %get-tuple-element.88), channel_id=1, source_target_pairs={{0,32},{1,33},{2,34},{3,35},{4,36},{5,37},{6,38},{7,39},{8,40},{9,... | collective-permute-start | bytes 1376264 | tf_op jit(solution)/shard_map/ppermute | solution.py:33
  102.5 5.9 %shard_map.67 = bf16[26,128,128]{2,1,0:T(8,128)(2,1)S(1)} custom-call(s32[5]{0:T(128)S(1)} %stack.23.at_ref, s32[40]{0:T(128)S(1)} %shard_map.62.pair_list_ref.list_ref, bf16[2,896,256]{2,1,0:T(8,128)(2,1)S(1)} %shard_map.63.refs_0_, bf16[2,896,256]{2,1,0:T(8,128)(2,1)S(1)} %collective-permute-done.10.refs_1_, ...), custom_call_target="tpu_custom_call" | custom-call | flops 20000000000 | bytes 100000000 | tf_op jit(solution)/shard_map/pallas_call | solution.py:67
  108.6 4.3 %collective-permute-done.22.low = bf16[2,64,1792]{2,1,0:T(8,128)(2,1)S(1)} collective-permute-done((bf16[2,64,1792]{2,1,0:T(8,128)(2,1)S(1)}, bf16[2,64,1792]{2,1,0:T(8,128)(2,1)S(1)}, u32[]{:S(2)}, u32[]{:S(2)}) %collective-permute-start.22) | collective-permute-done | bytes 458784 | tf_op jit(solution)/shard_map/ppermute | solution.py:33
  112.8 3.4 %collective-permute-done.23.high = bf16[2,64,1792]{2,1,0:T(8,128)(2,1)S(1)} collective-permute-done((bf16[2,64,1792]{2,1,0:T(8,128)(2,1)S(1)}, bf16[2,64,1792]{2,1,0:T(8,128)(2,1)S(1)}, u32[]{:S(2)}, u32[]{:S(2)}) %collective-permute-start.23) | collective-permute-done | bytes 458784 | tf_op jit(solution)/shard_map/ppermute | solution.py:33
  116.7 1.7 %collective-permute-start.25 = (bf16[128,1792]{1,0:T(8,128)(2,1)S(1)}, bf16[128,1792]{1,0:T(8,128)(2,1)S(1)}, u32[]{:S(2)}, u32[]{:S(2)}) collective-permute-start(bf16[128,1792]{1,0:T(8,128)(2,1)S(1)} %get-tuple-element.96), channel_id=1, source_target_pairs={{0,96},{1,97},{2,98},{3,99},{4,100},{5,101},{6,102},{7,103},{8,104... | collective-permute-start | bytes 1376264 | tf_op jit(solution)/shard_map/ppermute | solution.py:33
  118.6 1.6 %collective-permute-start.28 = (bf16[128,1792]{1,0:T(8,128)(2,1)S(1)}, bf16[128,1792]{1,0:T(8,128)(2,1)S(1)}, u32[]{:S(2)}, u32[]{:S(2)}) collective-permute-start(bf16[128,1792]{1,0:T(8,128)(2,1)S(1)} %get-tuple-element.93), channel_id=1, source_target_pairs={{0,32},{1,33},{2,34},{3,35},{4,36},{5,37},{6,38},{7,39},{8,40},{9,... | collective-permute-start | bytes 1376264 | tf_op jit(solution)/shard_map/ppermute | solution.py:33
  120.7 5.9 %shard_map.70.own_ref = f32[26,128,128]{2,1,0:T(8,128)S(1)} custom-call(s32[5]{0:T(128)S(1)} %stack.23.at_ref, s32[40]{0:T(128)S(1)} %get-tuple-element.60.list_ref, bf16[2,896,256]{2,1,0:T(8,128)(2,1)S(1)} %shard_map.63.refs_0_, bf16[2,896,256]{2,1,0:T(8,128)(2,1)S(1)} %collective-permute-done.10.refs_1_, ...), custom_call_target="tpu_custom_call" | custom-call | bytes 1024 | tf_op jit(solution)/shard_map/pallas_call | solution.py:67
  126.6 3.3 %collective-permute-done.24.up = bf16[128,1792]{1,0:T(8,128)(2,1)S(1)} collective-permute-done((bf16[128,1792]{1,0:T(8,128)(2,1)S(1)}, bf16[128,1792]{1,0:T(8,128)(2,1)S(1)}, u32[]{:S(2)}, u32[]{:S(2)}) %collective-permute-start.24) | collective-permute-done | bytes 458784 | tf_op jit(solution)/shard_map/ppermute | solution.py:33
  129.9 1.5 collective-permute-done.25.down
  131.4 0.8 shard_map.71
  132.3 3.2 %collective-permute-start.27 = (bf16[128,896]{1,0:T(8,128)(2,1)S(1)}, bf16[128,896]{1,0:T(8,128)(2,1)S(1)}, u32[]{:S(2)}, u32[]{:S(2)}) collective-permute-start(bf16[128,896]{1,0:T(8,128)(2,1)S(1)} %get-tuple-element.99), channel_id=1, source_target_pairs={{1,16},{3,18},{5,20},{7,22},{9,24},{11,26},{13,28},{15,30},{16,1},... | collective-permute-start | bytes 688136 | tf_op jit(solution)/shard_map/ppermute | solution.py:33
  135.5 2.8 %collective-permute-done.26.a0 = bf16[128,896]{1,0:T(8,128)(2,1)S(1)} collective-permute-done((bf16[128,896]{1,0:T(8,128)(2,1)S(1)}, bf16[128,896]{1,0:T(8,128)(2,1)S(1)}, u32[]{:S(2)}, u32[]{:S(2)}) %collective-permute-start.26) | collective-permute-done | bytes 229408 | tf_op jit(solution)/shard_map/ppermute | solution.py:33
  138.3 1.9 %collective-permute-done.27.b0 = bf16[128,896]{1,0:T(8,128)(2,1)S(1)} collective-permute-done((bf16[128,896]{1,0:T(8,128)(2,1)S(1)}, bf16[128,896]{1,0:T(8,128)(2,1)S(1)}, u32[]{:S(2)}, u32[]{:S(2)}) %collective-permute-start.27) | collective-permute-done | bytes 229408 | tf_op jit(solution)/shard_map/ppermute | solution.py:33
  140.2 0.8 shard_map.72
  141.1 3.2 %collective-permute-start.31 = (bf16[128,896]{1,0:T(8,128)(2,1)S(1)}, bf16[128,896]{1,0:T(8,128)(2,1)S(1)}, u32[]{:S(2)}, u32[]{:S(2)}) collective-permute-start(bf16[128,896]{1,0:T(8,128)(2,1)S(1)} %get-tuple-element.105), channel_id=1, source_target_pairs={{1,16},{3,18},{5,20},{7,22},{9,24},{11,26},{13,28},{15,30},{16,1},... | collective-permute-start | bytes 688136 | tf_op jit(solution)/shard_map/ppermute | solution.py:33
  144.3 3.0 %shard_map.74 = bf16[896,1792]{1,0:T(8,128)(2,1)} custom-call(s32[40]{0:T(128)S(1)} %get-tuple-element.60.list_ref, f32[26,128,128]{2,1,0:T(8,128)S(1)} %shard_map.70.own_ref, bf16[26,128,128]{2,1,0:T(8,128)(2,1)S(1)} %collective-permute-done.32.got_ref), custom_call_target="tpu_custom_call" | custom-call | flops 10000000000 | bytes 50000000 | tf_op jit(solution)/shard_map/pallas_call | solution.py:67
  147.2 1.8 %collective-permute-done.31.b1 = bf16[128,896]{1,0:T(8,128)(2,1)S(1)} collective-permute-done((bf16[128,896]{1,0:T(8,128)(2,1)S(1)}, bf16[128,896]{1,0:T(8,128)(2,1)S(1)}, u32[]{:S(2)}, u32[]{:S(2)}) %collective-permute-start.31) | collective-permute-done | bytes 229408 | tf_op jit(solution)/shard_map/ppermute | solution.py:33
  149.0 1.4 shard_map.73
  (47 shorter events, 3.6 us)
Async XLA Ops:
  0.7 1.0 copy-start.2
  2.5 9.2 %collective-permute-start.1 = (bf16[32,1792]{1,0:T(8,128)(2,1)S(1)}, bf16[32,1792]{1,0:T(8,128)(2,1)S(1)}, u32[]{:S(2)}, u32[]{:S(2)}) collective-permute-start(bf16[32,1792]{1,0:T(8,128)(2,1)S(1)} %get-tuple-element.56), channel_id=1, source_target_pairs={{0,6},{1,7},{2,0},{3,1},{4,2},{5,3},{6,4},{7,5},{8,14},{9,15},{10,... | collective-permute-start | bytes 344072 | tf_op jit(solution)/shard_map/ppermute | solution.py:33
  6.6 7.4 %collective-permute-start.2 = (bf16[32,1792]{1,0:T(8,128)(2,1)S(1)}, bf16[32,1792]{1,0:T(8,128)(2,1)S(1)}, u32[]{:S(2)}, u32[]{:S(2)}) collective-permute-start(bf16[32,1792]{1,0:T(8,128)(2,1)S(1)} %get-tuple-element.57), channel_id=1, source_target_pairs={{0,4},{1,5},{2,6},{3,7},{4,0},{5,1},{6,2},{7,3},{8,12},{9,13},{10,... | collective-permute-start | bytes 344072 | tf_op jit(solution)/shard_map/ppermute | solution.py:33
  6.6 8.3 %collective-permute-start.3 = (bf16[32,1792]{1,0:T(8,128)(2,1)S(1)}, bf16[32,1792]{1,0:T(8,128)(2,1)S(1)}, u32[]{:S(2)}, u32[]{:S(2)}) collective-permute-start(bf16[32,1792]{1,0:T(8,128)(2,1)S(1)} %get-tuple-element.58), channel_id=1, source_target_pairs={{0,2},{1,3},{2,4},{3,5},{4,6},{5,7},{6,0},{7,1},{8,10},{9,11},{10,... | collective-permute-start | bytes 344072 | tf_op jit(solution)/shard_map/ppermute | solution.py:33
  7.9 3.8 %collective-permute-start = (s32[7,14]{1,0:T(8,128)}, s32[7,14]{1,0:T(8,128)S(1)}, u32[]{:S(2)}, u32[]{:S(2)}) collective-permute-start(s32[7,14]{1,0:T(8,128)} %mask_ref), channel_id=1, source_target_pairs={{0,1},{1,0},{2,3},{3,2},{4,5},{5,4},{6,7},{7,6},{8,9},{9,8},{10,11... | collective-permute-start | bytes 1184 | tf_op jit(solution)/shard_map/ppermute | solution.py:33
  16.1 13.8 %collective-permute-start.7 = (bf16[4,32,1792]{2,1,0:T(8,128)(2,1)S(1)}, bf16[4,32,1792]{2,1,0:T(8,128)(2,1)S(1)}, u32[]{:S(2)}, u32[]{:S(2)}) collective-permute-start(bf16[4,32,1792]{2,1,0:T(8,128)(2,1)S(1)} %shard_map.60.mine), channel_id=1, source_target_pairs={{0,16},{1,0},{2,18},{3,2},{4,20},{5,4},{6,22},{7,6},{8,24},{9,8},{... | collective-permute-start | bytes 1376264 | tf_op jit(solution)/shard_map/ppermute | solution.py:33
  16.7 22.9 %collective-permute-start.8 = (bf16[4,32,1792]{2,1,0:T(8,128)(2,1)S(1)}, bf16[4,32,1792]{2,1,0:T(8,128)(2,1)S(1)}, u32[]{:S(2)}, u32[]{:S(2)}) collective-permute-start(bf16[4,32,1792]{2,1,0:T(8,128)(2,1)S(1)} %shard_map.60.mine), channel_id=1, source_target_pairs={{1,16},{3,18},{5,20},{7,22},{9,24},{11,26},{13,28},{15,30},{16,1},... | collective-permute-start | bytes 1376264 | tf_op jit(solution)/shard_map/ppermute | solution.py:33
  20.8 44.1 %collective-permute-start.5 = (bf16[512,1792]{1,0:T(8,128)(2,1)}, bf16[512,1792]{1,0:T(8,128)(2,1)S(1)}, u32[]{:S(2)}, u32[]{:S(2)}) collective-permute-start(bf16[512,1792]{1,0:T(8,128)(2,1)} %refs_10_.3), channel_id=1, source_target_pairs={{0,6},{1,7},{2,0},{3,1},{4,2},{5,3},{6,4},{7,5},{8,14},{9,15},{10,... | collective-permute-start | bytes 5505032 | tf_op jit(solution)/shard_map/ppermute | solution.py:33
  21.7 42.9 %collective-permute-start.6 = (bf16[512,1792]{1,0:T(8,128)(2,1)}, bf16[512,1792]{1,0:T(8,128)(2,1)S(1)}, u32[]{:S(2)}, u32[]{:S(2)}) collective-permute-start(bf16[512,1792]{1,0:T(8,128)(2,1)} %refs_10_.3), channel_id=1, source_target_pairs={{0,2},{1,3},{2,4},{3,5},{4,6},{5,7},{6,0},{7,1},{8,10},{9,11},{10,... | collective-permute-start | bytes 5505032 | tf_op jit(solution)/shard_map/ppermute | solution.py:33
  22.9 1.9 %copy-start = (bf16[896,1792]{1,0:T(8,128)(2,1)S(1)}, bf16[896,1792]{1,0:T(8,128)(2,1)}, u32[]{:S(2)}) copy-start(bf16[896,1792]{1,0:T(8,128)(2,1)} %w_ref.1) | copy-start | bytes 9633796
  24.8 0.7 copy-start.3
  29.9 19.5 %collective-permute-start.4 = (bf16[26,128,128]{2,1,0:T(8,128)(2,1)S(1)}, bf16[26,128,128]{2,1,0:T(8,128)(2,1)S(1)}, u32[]{:S(2)}, u32[]{:S(2)}) collective-permute-start(bf16[26,128,128]{2,1,0:T(8,128)(2,1)S(1)} %get-tuple-element.61.blocks_ref), channel_id=1, source_target_pairs={{0,1},{1,0},{2,3},{3,2},{4,5},{5,4},{6,7},{7,6},{8,9},{9,8},{10,11... | collective-permute-start | bytes 2555912 | tf_op jit(solution)/shard_map/ppermute | solution.py:33
  40.5 23.6 %collective-permute-start.10 = (bf16[2,896,256]{2,1,0:T(8,128)(2,1)S(1)}, bf16[2,896,256]{2,1,0:T(8,128)(2,1)S(1)}, u32[]{:S(2)}, u32[]{:S(2)}) collective-permute-start(bf16[2,896,256]{2,1,0:T(8,128)(2,1)S(1)} %shard_map.63.refs_0_), channel_id=1, source_target_pairs={{0,96},{1,97},{2,98},{3,99},{4,100},{5,101},{6,102},{7,103},{8,104... | collective-permute-start | bytes 2752520 | tf_op jit(solution)/shard_map/ppermute | solution.py:33
  41.3 22.7 %collective-permute-start.12 = (bf16[2,896,256]{2,1,0:T(8,128)(2,1)S(1)}, bf16[2,896,256]{2,1,0:T(8,128)(2,1)S(1)}, u32[]{:S(2)}, u32[]{:S(2)}) collective-permute-start(bf16[2,896,256]{2,1,0:T(8,128)(2,1)S(1)} %shard_map.63.refs_0_), channel_id=1, source_target_pairs={{0,32},{1,33},{2,34},{3,35},{4,36},{5,37},{6,38},{7,39},{8,40},{9,... | collective-permute-start | bytes 2752520 | tf_op jit(solution)/shard_map/ppermute | solution.py:33
  51.4 19.4 %copy-start.1 = (bf16[512,1792]{1,0:T(8,128)(2,1)S(1)}, bf16[512,1792]{1,0:T(8,128)(2,1)}, u32[]{:S(2)}) copy-start(bf16[512,1792]{1,0:T(8,128)(2,1)} %refs_10_.3) | copy-start | bytes 5505028
  51.4 16.8 %collective-permute-start.9 = (bf16[2,896,256]{2,1,0:T(8,128)(2,1)S(1)}, bf16[2,896,256]{2,1,0:T(8,128)(2,1)S(1)}, u32[]{:S(2)}, u32[]{:S(2)}) collective-permute-start(bf16[2,896,256]{2,1,0:T(8,128)(2,1)S(1)} %shard_map.63.refs_0_), channel_id=1, source_target_pairs={{0,8},{1,9},{2,10},{3,11},{4,12},{5,13},{6,14},{7,15},{8,0},{9,1},... | collective-permute-start | bytes 2752520 | tf_op jit(solution)/shard_map/ppermute | solution.py:33
  64.1 4.1 %collective-permute-start.11 = (bf16[2,896,256]{2,1,0:T(8,128)(2,1)S(1)}, bf16[2,896,256]{2,1,0:T(8,128)(2,1)S(1)}, u32[]{:S(2)}, u32[]{:S(2)}) collective-permute-start(bf16[2,896,256]{2,1,0:T(8,128)(2,1)S(1)} %collective-permute-done.10.refs_1_), channel_id=1, source_target_pairs={{0,8},{1,9},{2,10},{3,11},{4,12},{5,13},{6,14},{7,15},{8,0},{9,1},... | collective-permute-start | bytes 2752520 | tf_op jit(solution)/shard_map/ppermute | solution.py:33
  64.1 4.1 %collective-permute-start.13 = (bf16[2,896,256]{2,1,0:T(8,128)(2,1)S(1)}, bf16[2,896,256]{2,1,0:T(8,128)(2,1)S(1)}, u32[]{:S(2)}, u32[]{:S(2)}) collective-permute-start(bf16[2,896,256]{2,1,0:T(8,128)(2,1)S(1)} %collective-permute-done.12.refs_2_), channel_id=1, source_target_pairs={{0,8},{1,9},{2,10},{3,11},{4,12},{5,13},{6,14},{7,15},{8,0},{9,1},... | collective-permute-start | bytes 2752520 | tf_op jit(solution)/shard_map/ppermute | solution.py:33
  64.7 23.5 %collective-permute-start.14 = (bf16[256,1792]{1,0:T(8,128)(2,1)S(1)}, bf16[256,1792]{1,0:T(8,128)(2,1)S(1)}, u32[]{:S(2)}, u32[]{:S(2)}) collective-permute-start(bf16[256,1792]{1,0:T(8,128)(2,1)S(1)} %slice.16), channel_id=1, source_target_pairs={{0,2},{1,3},{2,4},{3,5},{4,6},{5,7},{6,0},{7,1},{8,10},{9,11},{10,... | collective-permute-start | bytes 2752520 | tf_op jit(solution)/shard_map/ppermute | solution.py:33
  64.9 23.4 %collective-permute-start.15 = (bf16[256,1792]{1,0:T(8,128)(2,1)S(1)}, bf16[256,1792]{1,0:T(8,128)(2,1)S(1)}, u32[]{:S(2)}, u32[]{:S(2)}) collective-permute-start(bf16[256,1792]{1,0:T(8,128)(2,1)S(1)} %slice.17), channel_id=1, source_target_pairs={{0,6},{1,7},{2,0},{3,1},{4,2},{5,3},{6,4},{7,5},{8,14},{9,15},{10,... | collective-permute-start | bytes 2752520 | tf_op jit(solution)/shard_map/ppermute | solution.py:33
  68.2 20.1 %collective-permute-start.16 = (bf16[896,256]{1,0:T(8,128)(2,1)S(1)}, bf16[896,256]{1,0:T(8,128)(2,1)S(1)}, u32[]{:S(2)}, u32[]{:S(2)}) collective-permute-start(bf16[896,256]{1,0:T(8,128)(2,1)S(1)} %slice_bitcast_fusion.1), channel_id=1, source_target_pairs={{0,32},{1,33},{2,34},{3,35},{4,36},{5,37},{6,38},{7,39},{8,40},{9,... | collective-permute-start | bytes 1376264 | tf_op jit(solution)/shard_map/ppermute | solution.py:33
  70.7 17.6 %collective-permute-start.17 = (bf16[896,256]{1,0:T(8,128)(2,1)S(1)}, bf16[896,256]{1,0:T(8,128)(2,1)S(1)}, u32[]{:S(2)}, u32[]{:S(2)}) collective-permute-start(bf16[896,256]{1,0:T(8,128)(2,1)S(1)} %slice_bitcast_fusion), channel_id=1, source_target_pairs={{0,96},{1,97},{2,98},{3,99},{4,100},{5,101},{6,102},{7,103},{8,104... | collective-permute-start | bytes 1376264 | tf_op jit(solution)/shard_map/ppermute | solution.py:33
  88.3 9.4 %collective-permute-start.18 = (bf16[3,256,1792]{2,1,0:T(8,128)(2,1)S(1)}, bf16[3,256,1792]{2,1,0:T(8,128)(2,1)S(1)}, u32[]{:S(2)}, u32[]{:S(2)}) collective-permute-start(bf16[3,256,1792]{2,1,0:T(8,128)(2,1)S(1)} %get-tuple-element.76), channel_id=1, source_target_pairs={{0,8},{1,9},{2,10},{3,11},{4,12},{5,13},{6,14},{7,15},{8,0},{9,1},... | collective-permute-start | bytes 8257544 | tf_op jit(solution)/shard_map/ppermute | solution.py:33
  94.7 3.0 %collective-permute-start.19 = (bf16[1,256,1792]{2,1,0:T(8,128)(2,1)S(1)}, bf16[1,256,1792]{2,1,0:T(8,128)(2,1)S(1)}, u32[]{:S(2)}, u32[]{:S(2)}) collective-permute-start(bf16[1,256,1792]{2,1,0:T(8,128)(2,1)S(1)} %get-tuple-element.77), channel_id=1, source_target_pairs={{0,8},{1,9},{2,10},{3,11},{4,12},{5,13},{6,14},{7,15},{8,0},{9,1},... | collective-permute-start | bytes 2752520 | tf_op jit(solution)/shard_map/ppermute | solution.py:33
  95.6 7.0 %collective-permute-start.20 = (bf16[896,256]{1,0:T(8,128)(2,1)S(1)}, bf16[896,256]{1,0:T(8,128)(2,1)S(1)}, u32[]{:S(2)}, u32[]{:S(2)}) collective-permute-start(bf16[896,256]{1,0:T(8,128)(2,1)S(1)} %collective-permute-done.16.refs_3_), channel_id=1, source_target_pairs={{0,8},{1,9},{2,10},{3,11},{4,12},{5,13},{6,14},{7,15},{8,0},{9,1},... | collective-permute-start | bytes 1376264 | tf_op jit(solution)/shard_map/ppermute | solution.py:33
  95.8 6.7 %collective-permute-start.21 = (bf16[896,256]{1,0:T(8,128)(2,1)S(1)}, bf16[896,256]{1,0:T(8,128)(2,1)S(1)}, u32[]{:S(2)}, u32[]{:S(2)}) collective-permute-start(bf16[896,256]{1,0:T(8,128)(2,1)S(1)} %collective-permute-done.17.refs_4_), channel_id=1, source_target_pairs={{0,8},{1,9},{2,10},{3,11},{4,12},{5,13},{6,14},{7,15},{8,0},{9,1},... | collective-permute-start | bytes 1376264 | tf_op jit(solution)/shard_map/ppermute | solution.py:33
  99.1 13.8 %collective-permute-start.22 = (bf16[2,64,1792]{2,1,0:T(8,128)(2,1)S(1)}, bf16[2,64,1792]{2,1,0:T(8,128)(2,1)S(1)}, u32[]{:S(2)}, u32[]{:S(2)}) collective-permute-start(bf16[2,64,1792]{2,1,0:T(8,128)(2,1)S(1)} %get-tuple-element.88), channel_id=1, source_target_pairs={{0,32},{1,33},{2,34},{3,35},{4,36},{5,37},{6,38},{7,39},{8,40},{9,... | collective-permute-start | bytes 1376264 | tf_op jit(solution)/shard_map/ppermute | solution.py:33
  102.5 13.7 %collective-permute-start.23 = (bf16[2,64,1792]{2,1,0:T(8,128)(2,1)S(1)}, bf16[2,64,1792]{2,1,0:T(8,128)(2,1)S(1)}, u32[]{:S(2)}, u32[]{:S(2)}) collective-permute-start(bf16[2,64,1792]{2,1,0:T(8,128)(2,1)S(1)} %get-tuple-element.89), channel_id=1, source_target_pairs={{0,96},{1,97},{2,98},{3,99},{4,100},{5,101},{6,102},{7,103},{8,104... | collective-permute-start | bytes 1376264 | tf_op jit(solution)/shard_map/ppermute | solution.py:33
  108.5 35.8 %collective-permute-start.32 = (bf16[26,128,128]{2,1,0:T(8,128)(2,1)S(1)}, bf16[26,128,128]{2,1,0:T(8,128)(2,1)S(1)}, u32[]{:S(2)}, u32[]{:S(2)}) collective-permute-start(bf16[26,128,128]{2,1,0:T(8,128)(2,1)S(1)} %shard_map.67), channel_id=1, source_target_pairs={{0,1},{1,0},{2,3},{3,2},{4,5},{5,4},{6,7},{7,6},{8,9},{9,8},{10,11... | collective-permute-start | bytes 2555912 | tf_op jit(solution)/shard_map/ppermute | solution.py:33
  116.4 13.5 %collective-permute-start.24 = (bf16[128,1792]{1,0:T(8,128)(2,1)S(1)}, bf16[128,1792]{1,0:T(8,128)(2,1)S(1)}, u32[]{:S(2)}, u32[]{:S(2)}) collective-permute-start(bf16[128,1792]{1,0:T(8,128)(2,1)S(1)} %get-tuple-element.90), channel_id=1, source_target_pairs={{0,32},{1,33},{2,34},{3,35},{4,36},{5,37},{6,38},{7,39},{8,40},{9,... | collective-permute-start | bytes 1376264 | tf_op jit(solution)/shard_map/ppermute | solution.py:33
  116.7 14.7 %collective-permute-start.25 = (bf16[128,1792]{1,0:T(8,128)(2,1)S(1)}, bf16[128,1792]{1,0:T(8,128)(2,1)S(1)}, u32[]{:S(2)}, u32[]{:S(2)}) collective-permute-start(bf16[128,1792]{1,0:T(8,128)(2,1)S(1)} %get-tuple-element.96), channel_id=1, source_target_pairs={{0,96},{1,97},{2,98},{3,99},{4,100},{5,101},{6,102},{7,103},{8,104... | collective-permute-start | bytes 1376264 | tf_op jit(solution)/shard_map/ppermute | solution.py:33
  118.6 21.6 %collective-permute-start.28 = (bf16[128,1792]{1,0:T(8,128)(2,1)S(1)}, bf16[128,1792]{1,0:T(8,128)(2,1)S(1)}, u32[]{:S(2)}, u32[]{:S(2)}) collective-permute-start(bf16[128,1792]{1,0:T(8,128)(2,1)S(1)} %get-tuple-element.93), channel_id=1, source_target_pairs={{0,32},{1,33},{2,34},{3,35},{4,36},{5,37},{6,38},{7,39},{8,40},{9,... | collective-permute-start | bytes 1376264 | tf_op jit(solution)/shard_map/ppermute | solution.py:33
  120.2 20.0 %collective-permute-start.29 = (bf16[128,1792]{1,0:T(8,128)(2,1)S(1)}, bf16[128,1792]{1,0:T(8,128)(2,1)S(1)}, u32[]{:S(2)}, u32[]{:S(2)}) collective-permute-start(bf16[128,1792]{1,0:T(8,128)(2,1)S(1)} %get-tuple-element.102), channel_id=1, source_target_pairs={{0,96},{1,97},{2,98},{3,99},{4,100},{5,101},{6,102},{7,103},{8,104... | collective-permute-start | bytes 1376264 | tf_op jit(solution)/shard_map/ppermute | solution.py:33
  132.2 6.1 %collective-permute-start.26 = (bf16[128,896]{1,0:T(8,128)(2,1)S(1)}, bf16[128,896]{1,0:T(8,128)(2,1)S(1)}, u32[]{:S(2)}, u32[]{:S(2)}) collective-permute-start(bf16[128,896]{1,0:T(8,128)(2,1)S(1)} %get-tuple-element.98), channel_id=1, source_target_pairs={{0,1},{1,17},{2,3},{3,19},{4,5},{5,21},{6,7},{7,23},{8,9},{9,25},{... | collective-permute-start | bytes 688136 | tf_op jit(solution)/shard_map/ppermute | solution.py:33
  132.3 7.9 %collective-permute-start.27 = (bf16[128,896]{1,0:T(8,128)(2,1)S(1)}, bf16[128,896]{1,0:T(8,128)(2,1)S(1)}, u32[]{:S(2)}, u32[]{:S(2)}) collective-permute-start(bf16[128,896]{1,0:T(8,128)(2,1)S(1)} %get-tuple-element.99), channel_id=1, source_target_pairs={{1,16},{3,18},{5,20},{7,22},{9,24},{11,26},{13,28},{15,30},{16,1},... | collective-permute-start | bytes 688136 | tf_op jit(solution)/shard_map/ppermute | solution.py:33
  141.0 6.2 %collective-permute-start.30 = (bf16[128,896]{1,0:T(8,128)(2,1)S(1)}, bf16[128,896]{1,0:T(8,128)(2,1)S(1)}, u32[]{:S(2)}, u32[]{:S(2)}) collective-permute-start(bf16[128,896]{1,0:T(8,128)(2,1)S(1)} %get-tuple-element.104), channel_id=1, source_target_pairs={{0,1},{1,17},{2,3},{3,19},{4,5},{5,21},{6,7},{7,23},{8,9},{9,25},{... | collective-permute-start | bytes 688136 | tf_op jit(solution)/shard_map/ppermute | solution.py:33
  141.1 7.9 %collective-permute-start.31 = (bf16[128,896]{1,0:T(8,128)(2,1)S(1)}, bf16[128,896]{1,0:T(8,128)(2,1)S(1)}, u32[]{:S(2)}, u32[]{:S(2)}) collective-permute-start(bf16[128,896]{1,0:T(8,128)(2,1)S(1)} %get-tuple-element.105), channel_id=1, source_target_pairs={{1,16},{3,18},{5,20},{7,22},{9,24},{11,26},{13,28},{15,30},{16,1},... | collective-permute-start | bytes 688136 | tf_op jit(solution)/shard_map/ppermute | solution.py:33

commit v2 on v1

--- a/solution.py
+++ b/solution.py
@@ -186,11 +186,10 @@
 
 def partial_kernel(count, at_ref, list_ref, pair_list_ref, blocks_ref, pair_blocks_ref, *refs):
     co = at_ref[CO]
-    g_refs, refs = refs[:-9], refs[-9:]
-    keep_ref, give_ref, blocks, grows, total, sums, g_sems, w_sems, o_sems = refs
+    g_refs, refs = refs[:-7], refs[-7:]
+    keep_ref, give_ref, grows, total, sums, g_sems, o_sems = refs
     toks, depth = sums.shape[2], sums.shape[3] // 2
     loads = move(stacked(g_refs, grows), g_sems)
-    loads += move([(blocks_ref, blocks.at[0]), (pair_blocks_ref, blocks.at[1])], w_sems)
     for load in loads:
         load.wait()
 
@@ -198,7 +197,8 @@
         return grows[:, span(place & 15)]
 
     stores = []
-    for tile, slots in enumerate((list_ref, pair_list_ref)):
+    sides = ((list_ref, blocks_ref), (pair_list_ref, pair_blocks_ref))
+    for tile, (slots, blocks) in enumerate(sides):
 
         def row(i, _):
             first, end = slots[ROWS + i], slots[ROWS + i + 1]
@@ -206,7 +206,7 @@
 
             def add(slot, size):
                 left = [rows_of(slots[slot + n]) for n in range(size)]
-                right = blocks[tile, pl.ds(slot, size)].reshape(size * BLK, BLK)
+                right = blocks[pl.ds(slot, size)].reshape(size * BLK, BLK)
                 total[...] += jnp.dot(
                     jnp.concatenate(left, axis=1), right, preferred_element_type=F32
                 )
@@ -406,15 +406,14 @@
     def partials(*grads, flops=0):
         count = sum(grad.shape[0] for grad in grads) // (2 * chunk)
         return call(
-            functools.partial(partial_kernel, count), [SMEM] * 3 + [ANY] * (2 + len(grads)),
+            functools.partial(partial_kernel, count), [SMEM] * 3 + [VMEM] * 2 + [ANY] * len(grads),
             [(out((count, chunk, wide)), ANY)] * 2,
             (place, slots, pair_slots, blocks, pair_blocks) + grads,
             [
-                pltpu.VMEM((2, CAP, BLK, BLK), BF16),
                 pltpu.VMEM((2 * count * chunk, hidden), BF16),
                 pltpu.VMEM((2 * count * chunk, BLK), F32),
                 pltpu.VMEM((2, count, chunk, wide), BF16),
-                dma((len(grads),)), dma((2,)), dma((4,)),
+                dma((len(grads),)), dma((4,)),
             ],
             flops=flops,
         )
@@ -487,7 +486,7 @@
         got_a = send(to_a, along_x({0: 1, 2: 0, 1: 3, 3: 2}))
         got_b = send(to_b, along_x({2: 1, 1: 2}))
         parts += (mine, got_a, got_b)
-        last = (got_a, got_b)
+        last = got_a
 
     (grad_weight,) = call(
         combine_kernel, [SMEM, VMEM, VMEM], [(out(weight.shape), VMEM)], (slots, own_sum, pair_got),

time: 151 us -> 149 us (0.987)
  transfers between devices with their start and end apart: 33 -> 33, of which waited for: 15 -> 15; matrix products, arithmetic and copies ran while one was open for 0% -> 0% of each run, Pallas kernels for 28% -> 27%
where the time goes in v2:
time: 149 us; the launch traced here: 148 us
  waiting for transfers between devices  61.6 us (41%)
  Pallas kernels  43.8 us (29%)
  starting transfers between devices  38.2 us (26%)
  local copies, waits for them, and re-layouts  3.89 us (3%)
    ppermute x33, waiting for transfers between devices, send(): return lax.ppermute(value, AXES, pairs)  61.6 us
    pallas_call x16, Pallas kernels, call(): pl.pallas_call(kernel, out_shape=tuple((shape for shape, _ in outs)), in_...  43.8 us
    ppermute x33, starting transfers between devices, send(): return lax.ppermute(value, AXES, pairs)  38.2 us
    unnamed x8, local copies, waits for them, and re-layouts  3.62 us
  transfers between devices with their start and end apart: 33, of which 15 were waited for; matrix products, arithmetic and copies ran while one was open for 0% of the time, Pallas kernels for 27%

profile of v2, /device:TPU:26, one launch (start us, length us, event | category | flops | bytes accessed | tf_op | source)
XLA Modules:
  0.0 148.5 jit_solution(3691319924530292415)
XLA Ops:
  0.7 1.0 copy-done.2
  1.7 0.8 shard_map.59
  2.5 4.1 %collective-permute-start.1 = (bf16[32,1792]{1,0:T(8,128)(2,1)S(1)}, bf16[32,1792]{1,0:T(8,128)(2,1)S(1)}, u32[]{:S(2)}, u32[]{:S(2)}) collective-permute-start(bf16[32,1792]{1,0:T(8,128)(2,1)S(1)} %get-tuple-element.56), channel_id=1, source_target_pairs={{0,6},{1,7},{2,0},{3,1},{4,2},{5,3},{6,4},{7,5},{8,14},{9,15},{10,... | collective-permute-start | bytes 344072 | tf_op jit(solution)/shard_map/ppermute | solution.py:33
  6.6 1.3 collective-permute-start.3
  8.4 3.3 %collective-permute-done.mask_ref = s32[7,14]{1,0:T(8,128)S(1)} collective-permute-done((s32[7,14]{1,0:T(8,128)}, s32[7,14]{1,0:T(8,128)S(1)}, u32[]{:S(2)}, u32[]{:S(2)}) %collective-permute-start) | collective-permute-done | bytes 424 | tf_op jit(solution)/shard_map/ppermute | solution.py:33
  11.7 2.3 %collective-permute-done.2.x2 = bf16[32,1792]{1,0:T(8,128)(2,1)S(1)} collective-permute-done((bf16[32,1792]{1,0:T(8,128)(2,1)S(1)}, bf16[32,1792]{1,0:T(8,128)(2,1)S(1)}, u32[]{:S(2)}, u32[]{:S(2)}) %collective-permute-start.2) | collective-permute-done | bytes 114720 | tf_op jit(solution)/shard_map/ppermute | solution.py:33
  14.0 0.9 collective-permute-done.3.x3
  14.9 1.2 shard_map.60.mine
  16.1 0.6 collective-permute-start.7
  16.7 4.0 %collective-permute-start.8 = (bf16[4,32,1792]{2,1,0:T(8,128)(2,1)S(1)}, bf16[4,32,1792]{2,1,0:T(8,128)(2,1)S(1)}, u32[]{:S(2)}, u32[]{:S(2)}) collective-permute-start(bf16[4,32,1792]{2,1,0:T(8,128)(2,1)S(1)} %shard_map.60.mine), channel_id=1, source_target_pairs={{1,16},{3,18},{5,20},{7,22},{9,24},{11,26},{13,28},{15,30},{16,1},... | collective-permute-start | bytes 1376264 | tf_op jit(solution)/shard_map/ppermute | solution.py:33
  20.8 1.0 collective-permute-start.5
  21.7 1.1 collective-permute-start.6
  22.9 1.9 %copy-done = bf16[896,1792]{1,0:T(8,128)(2,1)S(1)} copy-done((bf16[896,1792]{1,0:T(8,128)(2,1)S(1)}, bf16[896,1792]{1,0:T(8,128)(2,1)}, u32[]{:S(2)}) %copy-start) | copy-done | bytes 3211288
  24.8 0.7 copy-done.3
  25.5 4.4 %shard_map.61 = (bf16[26,128,128]{2,1,0:T(8,128)(2,1)S(1)}, s32[40]{0:T(128)S(1)}) custom-call(s32[7,14]{1,0:T(8,128)S(1)} %copy-done.3, bf16[896,1792]{1,0:T(8,128)(2,1)S(1)} %copy-done), custom_call_target="tpu_custom_call" | custom-call | bytes 1024 | tf_op jit(solution)/shard_map/pallas_call | solution.py:67
  30.0 9.6 %collective-permute-done.8.got_b = bf16[4,32,1792]{2,1,0:T(8,128)(2,1)S(1)} collective-permute-done((bf16[4,32,1792]{2,1,0:T(8,128)(2,1)S(1)}, bf16[4,32,1792]{2,1,0:T(8,128)(2,1)S(1)}, u32[]{:S(2)}, u32[]{:S(2)}) %collective-permute-start.8) | collective-permute-done | bytes 458784 | tf_op jit(solution)/shard_map/ppermute | solution.py:33
  39.6 0.9 shard_map.63.refs_0_
  40.5 0.8 collective-permute-start.10
  41.3 2.5 %collective-permute-start.12 = (bf16[2,896,256]{2,1,0:T(8,128)(2,1)S(1)}, bf16[2,896,256]{2,1,0:T(8,128)(2,1)S(1)}, u32[]{:S(2)}, u32[]{:S(2)}) collective-permute-start(bf16[2,896,256]{2,1,0:T(8,128)(2,1)S(1)} %shard_map.63.refs_0_), channel_id=1, source_target_pairs={{0,32},{1,33},{2,34},{3,35},{4,36},{5,37},{6,38},{7,39},{8,40},{9,... | collective-permute-start | bytes 2752520 | tf_op jit(solution)/shard_map/ppermute | solution.py:33
  43.8 5.5 %collective-permute-done.4.pair_blocks_ref = bf16[26,128,128]{2,1,0:T(8,128)(2,1)S(1)} collective-permute-done((bf16[26,128,128]{2,1,0:T(8,128)(2,1)S(1)}, bf16[26,128,128]{2,1,0:T(8,128)(2,1)S(1)}, u32[]{:S(2)}, u32[]{:S(2)}) %collective-permute-start.4) | collective-permute-done | bytes 852000 | tf_op jit(solution)/shard_map/ppermute | solution.py:33
  49.3 2.0 %shard_map.62.pair_list_ref.list_ref = s32[40]{0:T(128)S(1)} custom-call(s32[7,14]{1,0:T(8,128)S(1)} %collective-permute-done.mask_ref), custom_call_target="tpu_custom_call" | custom-call | flops 5000000000 | bytes 25000000 | tf_op jit(solution)/shard_map/pallas_call | solution.py:67
  51.5 12.6 %collective-permute-done.10.refs_1_ = bf16[2,896,256]{2,1,0:T(8,128)(2,1)S(1)} collective-permute-done((bf16[2,896,256]{2,1,0:T(8,128)(2,1)S(1)}, bf16[2,896,256]{2,1,0:T(8,128)(2,1)S(1)}, u32[]{:S(2)}, u32[]{:S(2)}) %collective-permute-start.10) | collective-permute-done | bytes 917536 | tf_op jit(solution)/shard_map/ppermute | solution.py:33
  64.9 3.3 %collective-permute-start.15 = (bf16[256,1792]{1,0:T(8,128)(2,1)S(1)}, bf16[256,1792]{1,0:T(8,128)(2,1)S(1)}, u32[]{:S(2)}, u32[]{:S(2)}) collective-permute-start(bf16[256,1792]{1,0:T(8,128)(2,1)S(1)} %slice.17), channel_id=1, source_target_pairs={{0,6},{1,7},{2,0},{3,1},{4,2},{5,3},{6,4},{7,5},{8,14},{9,15},{10,... | collective-permute-start | bytes 2752520 | tf_op jit(solution)/shard_map/ppermute | solution.py:33
  68.2 2.5 %collective-permute-start.16 = (bf16[896,256]{1,0:T(8,128)(2,1)S(1)}, bf16[896,256]{1,0:T(8,128)(2,1)S(1)}, u32[]{:S(2)}, u32[]{:S(2)}) collective-permute-start(bf16[896,256]{1,0:T(8,128)(2,1)S(1)} %slice_bitcast_fusion.1), channel_id=1, source_target_pairs={{0,32},{1,33},{2,34},{3,35},{4,36},{5,37},{6,38},{7,39},{8,40},{9,... | collective-permute-start | bytes 1376264 | tf_op jit(solution)/shard_map/ppermute | solution.py:33
  70.7 9.5 %shard_map.64 = (bf16[3,256,1792]{2,1,0:T(8,128)(2,1)S(1)}, bf16[3,256,1792]{2,1,0:T(8,128)(2,1)S(1)}) custom-call(s32[5]{0:T(128)S(1)} %stack.23.at_ref, s32[40]{0:T(128)S(1)} %get-tuple-element.60.list_ref, s32[40]{0:T(128)S(1)} %shard_map.62.pair_list_ref.list_ref, bf16[26,128,128]{2,1,0:T(8,128)(2,1)S(1)} %get-tuple-element.61.blocks_ref, ...), custom_call_target="tpu_custom_call" | custom-call | flops 10000000000 | bytes 50000000 | tf_op jit(solution)/shard_map/pallas_call | solution.py:67
  80.2 8.0 %collective-permute-done.14.refs_0_.refs_12_ = bf16[256,1792]{1,0:T(8,128)(2,1)S(1)} collective-permute-done((bf16[256,1792]{1,0:T(8,128)(2,1)S(1)}, bf16[256,1792]{1,0:T(8,128)(2,1)S(1)}, u32[]{:S(2)}, u32[]{:S(2)}) %collective-permute-start.14) | collective-permute-done | bytes 917536 | tf_op jit(solution)/shard_map/ppermute | solution.py:33
  88.4 5.6 %shard_map.65 = (bf16[1,256,1792]{2,1,0:T(8,128)(2,1)S(1)}, bf16[1,256,1792]{2,1,0:T(8,128)(2,1)S(1)}) custom-call(s32[5]{0:T(128)S(1)} %stack.23.at_ref, s32[40]{0:T(128)S(1)} %get-tuple-element.60.list_ref, s32[40]{0:T(128)S(1)} %shard_map.62.pair_list_ref.list_ref, bf16[26,128,128]{2,1,0:T(8,128)(2,1)S(1)} %get-tuple-element.61.blocks_ref, ...), custom_call_target="tpu_custom_call" | custom-call | bytes 1024 | tf_op jit(solution)/shard_map/pallas_call | solution.py:67
  94.0 0.8 collective-permute-start.19
  95.3 1.6 %collective-permute-done.19.far_got = bf16[1,256,1792]{2,1,0:T(8,128)(2,1)S(1)} collective-permute-done((bf16[1,256,1792]{2,1,0:T(8,128)(2,1)S(1)}, bf16[1,256,1792]{2,1,0:T(8,128)(2,1)S(1)}, u32[]{:S(2)}, u32[]{:S(2)}) %collective-permute-start.19) | collective-permute-done | bytes 917536 | tf_op jit(solution)/shard_map/ppermute | solution.py:33
  96.9 1.4 shard_map.66
  98.3 2.7 %collective-permute-start.22 = (bf16[2,64,1792]{2,1,0:T(8,128)(2,1)S(1)}, bf16[2,64,1792]{2,1,0:T(8,128)(2,1)S(1)}, u32[]{:S(2)}, u32[]{:S(2)}) collective-permute-start(bf16[2,64,1792]{2,1,0:T(8,128)(2,1)S(1)} %get-tuple-element.88), channel_id=1, source_target_pairs={{0,32},{1,33},{2,34},{3,35},{4,36},{5,37},{6,38},{7,39},{8,40},{9,... | collective-permute-start | bytes 1376264 | tf_op jit(solution)/shard_map/ppermute | solution.py:33
  101.1 5.9 %shard_map.67 = bf16[26,128,128]{2,1,0:T(8,128)(2,1)S(1)} custom-call(s32[5]{0:T(128)S(1)} %stack.23.at_ref, s32[40]{0:T(128)S(1)} %shard_map.62.pair_list_ref.list_ref, bf16[2,896,256]{2,1,0:T(8,128)(2,1)S(1)} %shard_map.63.refs_0_, bf16[2,896,256]{2,1,0:T(8,128)(2,1)S(1)} %collective-permute-done.10.refs_1_, ...), custom_call_target="tpu_custom_call" | custom-call | flops 20000000000 | bytes 100000000 | tf_op jit(solution)/shard_map/pallas_call | solution.py:67
  107.1 4.2 %collective-permute-done.22.low = bf16[2,64,1792]{2,1,0:T(8,128)(2,1)S(1)} collective-permute-done((bf16[2,64,1792]{2,1,0:T(8,128)(2,1)S(1)}, bf16[2,64,1792]{2,1,0:T(8,128)(2,1)S(1)}, u32[]{:S(2)}, u32[]{:S(2)}) %collective-permute-start.22) | collective-permute-done | bytes 458784 | tf_op jit(solution)/shard_map/ppermute | solution.py:33
  111.4 3.4 %collective-permute-done.23.high = bf16[2,64,1792]{2,1,0:T(8,128)(2,1)S(1)} collective-permute-done((bf16[2,64,1792]{2,1,0:T(8,128)(2,1)S(1)}, bf16[2,64,1792]{2,1,0:T(8,128)(2,1)S(1)}, u32[]{:S(2)}, u32[]{:S(2)}) %collective-permute-start.23) | collective-permute-done | bytes 458784 | tf_op jit(solution)/shard_map/ppermute | solution.py:33
  115.2 1.7 %collective-permute-start.25 = (bf16[128,1792]{1,0:T(8,128)(2,1)S(1)}, bf16[128,1792]{1,0:T(8,128)(2,1)S(1)}, u32[]{:S(2)}, u32[]{:S(2)}) collective-permute-start(bf16[128,1792]{1,0:T(8,128)(2,1)S(1)} %get-tuple-element.96), channel_id=1, source_target_pairs={{0,96},{1,97},{2,98},{3,99},{4,100},{5,101},{6,102},{7,103},{8,104... | collective-permute-start | bytes 1376264 | tf_op jit(solution)/shard_map/ppermute | solution.py:33
  117.1 1.6 %collective-permute-start.28 = (bf16[128,1792]{1,0:T(8,128)(2,1)S(1)}, bf16[128,1792]{1,0:T(8,128)(2,1)S(1)}, u32[]{:S(2)}, u32[]{:S(2)}) collective-permute-start(bf16[128,1792]{1,0:T(8,128)(2,1)S(1)} %get-tuple-element.93), channel_id=1, source_target_pairs={{0,32},{1,33},{2,34},{3,35},{4,36},{5,37},{6,38},{7,39},{8,40},{9,... | collective-permute-start | bytes 1376264 | tf_op jit(solution)/shard_map/ppermute | solution.py:33
  119.2 5.9 %shard_map.70.own_ref = f32[26,128,128]{2,1,0:T(8,128)S(1)} custom-call(s32[5]{0:T(128)S(1)} %stack.23.at_ref, s32[40]{0:T(128)S(1)} %get-tuple-element.60.list_ref, bf16[2,896,256]{2,1,0:T(8,128)(2,1)S(1)} %shard_map.63.refs_0_, bf16[2,896,256]{2,1,0:T(8,128)(2,1)S(1)} %collective-permute-done.10.refs_1_, ...), custom_call_target="tpu_custom_call" | custom-call | bytes 1024 | tf_op jit(solution)/shard_map/pallas_call | solution.py:67
  125.1 3.3 %collective-permute-done.24.up = bf16[128,1792]{1,0:T(8,128)(2,1)S(1)} collective-permute-done((bf16[128,1792]{1,0:T(8,128)(2,1)S(1)}, bf16[128,1792]{1,0:T(8,128)(2,1)S(1)}, u32[]{:S(2)}, u32[]{:S(2)}) %collective-permute-start.24) | collective-permute-done | bytes 458784 | tf_op jit(solution)/shard_map/ppermute | solution.py:33
  128.4 1.5 %collective-permute-done.25.down = bf16[128,1792]{1,0:T(8,128)(2,1)S(1)} collective-permute-done((bf16[128,1792]{1,0:T(8,128)(2,1)S(1)}, bf16[128,1792]{1,0:T(8,128)(2,1)S(1)}, u32[]{:S(2)}, u32[]{:S(2)}) %collective-permute-start.25) | collective-permute-done | bytes 458784 | tf_op jit(solution)/shard_map/ppermute | solution.py:33
  129.9 0.8 shard_map.71
  130.8 3.4 %collective-permute-start.27 = (bf16[128,896]{1,0:T(8,128)(2,1)S(1)}, bf16[128,896]{1,0:T(8,128)(2,1)S(1)}, u32[]{:S(2)}, u32[]{:S(2)}) collective-permute-start(bf16[128,896]{1,0:T(8,128)(2,1)S(1)} %get-tuple-element.99), channel_id=1, source_target_pairs={{1,16},{3,18},{5,20},{7,22},{9,24},{11,26},{13,28},{15,30},{16,1},... | collective-permute-start | bytes 688136 | tf_op jit(solution)/shard_map/ppermute | solution.py:33
  134.2 2.6 %collective-permute-done.26.a0 = bf16[128,896]{1,0:T(8,128)(2,1)S(1)} collective-permute-done((bf16[128,896]{1,0:T(8,128)(2,1)S(1)}, bf16[128,896]{1,0:T(8,128)(2,1)S(1)}, u32[]{:S(2)}, u32[]{:S(2)}) %collective-permute-start.26) | collective-permute-done | bytes 229408 | tf_op jit(solution)/shard_map/ppermute | solution.py:33
  136.8 1.2 collective-permute-done.29.down
  138.0 0.8 shard_map.72
  139.2 3.4 %collective-permute-start.31 = (bf16[128,896]{1,0:T(8,128)(2,1)S(1)}, bf16[128,896]{1,0:T(8,128)(2,1)S(1)}, u32[]{:S(2)}, u32[]{:S(2)}) collective-permute-start(bf16[128,896]{1,0:T(8,128)(2,1)S(1)} %get-tuple-element.105), channel_id=1, source_target_pairs={{1,16},{3,18},{5,20},{7,22},{9,24},{11,26},{13,28},{15,30},{16,1},... | collective-permute-start | bytes 688136 | tf_op jit(solution)/shard_map/ppermute | solution.py:33
  142.6 3.0 %shard_map.74 = bf16[896,1792]{1,0:T(8,128)(2,1)} custom-call(s32[40]{0:T(128)S(1)} %get-tuple-element.60.list_ref, f32[26,128,128]{2,1,0:T(8,128)S(1)} %shard_map.70.own_ref, bf16[26,128,128]{2,1,0:T(8,128)(2,1)S(1)} %collective-permute-done.32.got_ref), custom_call_target="tpu_custom_call" | custom-call | flops 10000000000 | bytes 50000000 | tf_op jit(solution)/shard_map/pallas_call | solution.py:67
  145.6 1.5 %collective-permute-done.31.b1 = bf16[128,896]{1,0:T(8,128)(2,1)S(1)} collective-permute-done((bf16[128,896]{1,0:T(8,128)(2,1)S(1)}, bf16[128,896]{1,0:T(8,128)(2,1)S(1)}, u32[]{:S(2)}, u32[]{:S(2)}) %collective-permute-start.31) | collective-permute-done | bytes 229408 | tf_op jit(solution)/shard_map/ppermute | solution.py:33
  147.1 1.4 shard_map.73
  (47 shorter events, 3.9 us)
Async XLA Ops:
  0.7 1.0 copy-start.2
  2.5 9.2 %collective-permute-start.1 = (bf16[32,1792]{1,0:T(8,128)(2,1)S(1)}, bf16[32,1792]{1,0:T(8,128)(2,1)S(1)}, u32[]{:S(2)}, u32[]{:S(2)}) collective-permute-start(bf16[32,1792]{1,0:T(8,128)(2,1)S(1)} %get-tuple-element.56), channel_id=1, source_target_pairs={{0,6},{1,7},{2,0},{3,1},{4,2},{5,3},{6,4},{7,5},{8,14},{9,15},{10,... | collective-permute-start | bytes 344072 | tf_op jit(solution)/shard_map/ppermute | solution.py:33
  6.6 7.4 %collective-permute-start.2 = (bf16[32,1792]{1,0:T(8,128)(2,1)S(1)}, bf16[32,1792]{1,0:T(8,128)(2,1)S(1)}, u32[]{:S(2)}, u32[]{:S(2)}) collective-permute-start(bf16[32,1792]{1,0:T(8,128)(2,1)S(1)} %get-tuple-element.57), channel_id=1, source_target_pairs={{0,4},{1,5},{2,6},{3,7},{4,0},{5,1},{6,2},{7,3},{8,12},{9,13},{10,... | collective-permute-start | bytes 344072 | tf_op jit(solution)/shard_map/ppermute | solution.py:33
  6.6 8.3 %collective-permute-start.3 = (bf16[32,1792]{1,0:T(8,128)(2,1)S(1)}, bf16[32,1792]{1,0:T(8,128)(2,1)S(1)}, u32[]{:S(2)}, u32[]{:S(2)}) collective-permute-start(bf16[32,1792]{1,0:T(8,128)(2,1)S(1)} %get-tuple-element.58), channel_id=1, source_target_pairs={{0,2},{1,3},{2,4},{3,5},{4,6},{5,7},{6,0},{7,1},{8,10},{9,11},{10,... | collective-permute-start | bytes 344072 | tf_op jit(solution)/shard_map/ppermute | solution.py:33
  7.9 3.8 %collective-permute-start = (s32[7,14]{1,0:T(8,128)}, s32[7,14]{1,0:T(8,128)S(1)}, u32[]{:S(2)}, u32[]{:S(2)}) collective-permute-start(s32[7,14]{1,0:T(8,128)} %mask_ref), channel_id=1, source_target_pairs={{0,1},{1,0},{2,3},{3,2},{4,5},{5,4},{6,7},{7,6},{8,9},{9,8},{10,11... | collective-permute-start | bytes 1184 | tf_op jit(solution)/shard_map/ppermute | solution.py:33
  16.1 13.8 %collective-permute-start.7 = (bf16[4,32,1792]{2,1,0:T(8,128)(2,1)S(1)}, bf16[4,32,1792]{2,1,0:T(8,128)(2,1)S(1)}, u32[]{:S(2)}, u32[]{:S(2)}) collective-permute-start(bf16[4,32,1792]{2,1,0:T(8,128)(2,1)S(1)} %shard_map.60.mine), channel_id=1, source_target_pairs={{0,16},{1,0},{2,18},{3,2},{4,20},{5,4},{6,22},{7,6},{8,24},{9,8},{... | collective-permute-start | bytes 1376264 | tf_op jit(solution)/shard_map/ppermute | solution.py:33
  16.7 22.9 %collective-permute-start.8 = (bf16[4,32,1792]{2,1,0:T(8,128)(2,1)S(1)}, bf16[4,32,1792]{2,1,0:T(8,128)(2,1)S(1)}, u32[]{:S(2)}, u32[]{:S(2)}) collective-permute-start(bf16[4,32,1792]{2,1,0:T(8,128)(2,1)S(1)} %shard_map.60.mine), channel_id=1, source_target_pairs={{1,16},{3,18},{5,20},{7,22},{9,24},{11,26},{13,28},{15,30},{16,1},... | collective-permute-start | bytes 1376264 | tf_op jit(solution)/shard_map/ppermute | solution.py:33
  20.8 44.1 %collective-permute-start.5 = (bf16[512,1792]{1,0:T(8,128)(2,1)}, bf16[512,1792]{1,0:T(8,128)(2,1)S(1)}, u32[]{:S(2)}, u32[]{:S(2)}) collective-permute-start(bf16[512,1792]{1,0:T(8,128)(2,1)} %refs_10_.3), channel_id=1, source_target_pairs={{0,6},{1,7},{2,0},{3,1},{4,2},{5,3},{6,4},{7,5},{8,14},{9,15},{10,... | collective-permute-start | bytes 5505032 | tf_op jit(solution)/shard_map/ppermute | solution.py:33
  21.7 42.9 %collective-permute-start.6 = (bf16[512,1792]{1,0:T(8,128)(2,1)}, bf16[512,1792]{1,0:T(8,128)(2,1)S(1)}, u32[]{:S(2)}, u32[]{:S(2)}) collective-permute-start(bf16[512,1792]{1,0:T(8,128)(2,1)} %refs_10_.3), channel_id=1, source_target_pairs={{0,2},{1,3},{2,4},{3,5},{4,6},{5,7},{6,0},{7,1},{8,10},{9,11},{10,... | collective-permute-start | bytes 5505032 | tf_op jit(solution)/shard_map/ppermute | solution.py:33
  22.9 1.9 %copy-start = (bf16[896,1792]{1,0:T(8,128)(2,1)S(1)}, bf16[896,1792]{1,0:T(8,128)(2,1)}, u32[]{:S(2)}) copy-start(bf16[896,1792]{1,0:T(8,128)(2,1)} %w_ref.1) | copy-start | bytes 9633796
  24.8 0.7 copy-start.3
  29.9 19.5 %collective-permute-start.4 = (bf16[26,128,128]{2,1,0:T(8,128)(2,1)S(1)}, bf16[26,128,128]{2,1,0:T(8,128)(2,1)S(1)}, u32[]{:S(2)}, u32[]{:S(2)}) collective-permute-start(bf16[26,128,128]{2,1,0:T(8,128)(2,1)S(1)} %get-tuple-element.61.blocks_ref), channel_id=1, source_target_pairs={{0,1},{1,0},{2,3},{3,2},{4,5},{5,4},{6,7},{7,6},{8,9},{9,8},{10,11... | collective-permute-start | bytes 2555912 | tf_op jit(solution)/shard_map/ppermute | solution.py:33
  40.5 23.6 %collective-permute-start.10 = (bf16[2,896,256]{2,1,0:T(8,128)(2,1)S(1)}, bf16[2,896,256]{2,1,0:T(8,128)(2,1)S(1)}, u32[]{:S(2)}, u32[]{:S(2)}) collective-permute-start(bf16[2,896,256]{2,1,0:T(8,128)(2,1)S(1)} %shard_map.63.refs_0_), channel_id=1, source_target_pairs={{0,96},{1,97},{2,98},{3,99},{4,100},{5,101},{6,102},{7,103},{8,104... | collective-permute-start | bytes 2752520 | tf_op jit(solution)/shard_map/ppermute | solution.py:33
  41.3 22.7 %collective-permute-start.12 = (bf16[2,896,256]{2,1,0:T(8,128)(2,1)S(1)}, bf16[2,896,256]{2,1,0:T(8,128)(2,1)S(1)}, u32[]{:S(2)}, u32[]{:S(2)}) collective-permute-start(bf16[2,896,256]{2,1,0:T(8,128)(2,1)S(1)} %shard_map.63.refs_0_), channel_id=1, source_target_pairs={{0,32},{1,33},{2,34},{3,35},{4,36},{5,37},{6,38},{7,39},{8,40},{9,... | collective-permute-start | bytes 2752520 | tf_op jit(solution)/shard_map/ppermute | solution.py:33
  51.4 19.4 %copy-start.1 = (bf16[512,1792]{1,0:T(8,128)(2,1)S(1)}, bf16[512,1792]{1,0:T(8,128)(2,1)}, u32[]{:S(2)}) copy-start(bf16[512,1792]{1,0:T(8,128)(2,1)} %refs_10_.3) | copy-start | bytes 5505028
  51.4 16.8 %collective-permute-start.9 = (bf16[2,896,256]{2,1,0:T(8,128)(2,1)S(1)}, bf16[2,896,256]{2,1,0:T(8,128)(2,1)S(1)}, u32[]{:S(2)}, u32[]{:S(2)}) collective-permute-start(bf16[2,896,256]{2,1,0:T(8,128)(2,1)S(1)} %shard_map.63.refs_0_), channel_id=1, source_target_pairs={{0,8},{1,9},{2,10},{3,11},{4,12},{5,13},{6,14},{7,15},{8,0},{9,1},... | collective-permute-start | bytes 2752520 | tf_op jit(solution)/shard_map/ppermute | solution.py:33
  64.1 4.1 %collective-permute-start.11 = (bf16[2,896,256]{2,1,0:T(8,128)(2,1)S(1)}, bf16[2,896,256]{2,1,0:T(8,128)(2,1)S(1)}, u32[]{:S(2)}, u32[]{:S(2)}) collective-permute-start(bf16[2,896,256]{2,1,0:T(8,128)(2,1)S(1)} %collective-permute-done.10.refs_1_), channel_id=1, source_target_pairs={{0,8},{1,9},{2,10},{3,11},{4,12},{5,13},{6,14},{7,15},{8,0},{9,1},... | collective-permute-start | bytes 2752520 | tf_op jit(solution)/shard_map/ppermute | solution.py:33
  64.1 4.1 %collective-permute-start.13 = (bf16[2,896,256]{2,1,0:T(8,128)(2,1)S(1)}, bf16[2,896,256]{2,1,0:T(8,128)(2,1)S(1)}, u32[]{:S(2)}, u32[]{:S(2)}) collective-permute-start(bf16[2,896,256]{2,1,0:T(8,128)(2,1)S(1)} %collective-permute-done.12.refs_2_), channel_id=1, source_target_pairs={{0,8},{1,9},{2,10},{3,11},{4,12},{5,13},{6,14},{7,15},{8,0},{9,1},... | collective-permute-start | bytes 2752520 | tf_op jit(solution)/shard_map/ppermute | solution.py:33
  64.7 23.5 %collective-permute-start.14 = (bf16[256,1792]{1,0:T(8,128)(2,1)S(1)}, bf16[256,1792]{1,0:T(8,128)(2,1)S(1)}, u32[]{:S(2)}, u32[]{:S(2)}) collective-permute-start(bf16[256,1792]{1,0:T(8,128)(2,1)S(1)} %slice.16), channel_id=1, source_target_pairs={{0,2},{1,3},{2,4},{3,5},{4,6},{5,7},{6,0},{7,1},{8,10},{9,11},{10,... | collective-permute-start | bytes 2752520 | tf_op jit(solution)/shard_map/ppermute | solution.py:33
  64.9 23.4 %collective-permute-start.15 = (bf16[256,1792]{1,0:T(8,128)(2,1)S(1)}, bf16[256,1792]{1,0:T(8,128)(2,1)S(1)}, u32[]{:S(2)}, u32[]{:S(2)}) collective-permute-start(bf16[256,1792]{1,0:T(8,128)(2,1)S(1)} %slice.17), channel_id=1, source_target_pairs={{0,6},{1,7},{2,0},{3,1},{4,2},{5,3},{6,4},{7,5},{8,14},{9,15},{10,... | collective-permute-start | bytes 2752520 | tf_op jit(solution)/shard_map/ppermute | solution.py:33
  68.2 20.1 %collective-permute-start.16 = (bf16[896,256]{1,0:T(8,128)(2,1)S(1)}, bf16[896,256]{1,0:T(8,128)(2,1)S(1)}, u32[]{:S(2)}, u32[]{:S(2)}) collective-permute-start(bf16[896,256]{1,0:T(8,128)(2,1)S(1)} %slice_bitcast_fusion.1), channel_id=1, source_target_pairs={{0,32},{1,33},{2,34},{3,35},{4,36},{5,37},{6,38},{7,39},{8,40},{9,... | collective-permute-start | bytes 1376264 | tf_op jit(solution)/shard_map/ppermute | solution.py:33
  70.7 17.6 %collective-permute-start.17 = (bf16[896,256]{1,0:T(8,128)(2,1)S(1)}, bf16[896,256]{1,0:T(8,128)(2,1)S(1)}, u32[]{:S(2)}, u32[]{:S(2)}) collective-permute-start(bf16[896,256]{1,0:T(8,128)(2,1)S(1)} %slice_bitcast_fusion), channel_id=1, source_target_pairs={{0,96},{1,97},{2,98},{3,99},{4,100},{5,101},{6,102},{7,103},{8,104... | collective-permute-start | bytes 1376264 | tf_op jit(solution)/shard_map/ppermute | solution.py:33
  88.3 8.6 %collective-permute-start.18 = (bf16[3,256,1792]{2,1,0:T(8,128)(2,1)S(1)}, bf16[3,256,1792]{2,1,0:T(8,128)(2,1)S(1)}, u32[]{:S(2)}, u32[]{:S(2)}) collective-permute-start(bf16[3,256,1792]{2,1,0:T(8,128)(2,1)S(1)} %get-tuple-element.76), channel_id=1, source_target_pairs={{0,8},{1,9},{2,10},{3,11},{4,12},{5,13},{6,14},{7,15},{8,0},{9,1},... | collective-permute-start | bytes 8257544 | tf_op jit(solution)/shard_map/ppermute | solution.py:33
  94.0 2.9 %collective-permute-start.19 = (bf16[1,256,1792]{2,1,0:T(8,128)(2,1)S(1)}, bf16[1,256,1792]{2,1,0:T(8,128)(2,1)S(1)}, u32[]{:S(2)}, u32[]{:S(2)}) collective-permute-start(bf16[1,256,1792]{2,1,0:T(8,128)(2,1)S(1)} %get-tuple-element.77), channel_id=1, source_target_pairs={{0,8},{1,9},{2,10},{3,11},{4,12},{5,13},{6,14},{7,15},{8,0},{9,1},... | collective-permute-start | bytes 2752520 | tf_op jit(solution)/shard_map/ppermute | solution.py:33
  94.8 6.3 %collective-permute-start.20 = (bf16[896,256]{1,0:T(8,128)(2,1)S(1)}, bf16[896,256]{1,0:T(8,128)(2,1)S(1)}, u32[]{:S(2)}, u32[]{:S(2)}) collective-permute-start(bf16[896,256]{1,0:T(8,128)(2,1)S(1)} %collective-permute-done.16.refs_3_), channel_id=1, source_target_pairs={{0,8},{1,9},{2,10},{3,11},{4,12},{5,13},{6,14},{7,15},{8,0},{9,1},... | collective-permute-start | bytes 1376264 | tf_op jit(solution)/shard_map/ppermute | solution.py:33
  95.1 6.0 %collective-permute-start.21 = (bf16[896,256]{1,0:T(8,128)(2,1)S(1)}, bf16[896,256]{1,0:T(8,128)(2,1)S(1)}, u32[]{:S(2)}, u32[]{:S(2)}) collective-permute-start(bf16[896,256]{1,0:T(8,128)(2,1)S(1)} %collective-permute-done.17.refs_4_), channel_id=1, source_target_pairs={{0,8},{1,9},{2,10},{3,11},{4,12},{5,13},{6,14},{7,15},{8,0},{9,1},... | collective-permute-start | bytes 1376264 | tf_op jit(solution)/shard_map/ppermute | solution.py:33
  98.3 13.1 %collective-permute-start.22 = (bf16[2,64,1792]{2,1,0:T(8,128)(2,1)S(1)}, bf16[2,64,1792]{2,1,0:T(8,128)(2,1)S(1)}, u32[]{:S(2)}, u32[]{:S(2)}) collective-permute-start(bf16[2,64,1792]{2,1,0:T(8,128)(2,1)S(1)} %get-tuple-element.88), channel_id=1, source_target_pairs={{0,32},{1,33},{2,34},{3,35},{4,36},{5,37},{6,38},{7,39},{8,40},{9,... | collective-permute-start | bytes 1376264 | tf_op jit(solution)/shard_map/ppermute | solution.py:33
  101.1 13.7 %collective-permute-start.23 = (bf16[2,64,1792]{2,1,0:T(8,128)(2,1)S(1)}, bf16[2,64,1792]{2,1,0:T(8,128)(2,1)S(1)}, u32[]{:S(2)}, u32[]{:S(2)}) collective-permute-start(bf16[2,64,1792]{2,1,0:T(8,128)(2,1)S(1)} %get-tuple-element.89), channel_id=1, source_target_pairs={{0,96},{1,97},{2,98},{3,99},{4,100},{5,101},{6,102},{7,103},{8,104... | collective-permute-start | bytes 1376264 | tf_op jit(solution)/shard_map/ppermute | solution.py:33
  107.0 35.6 %collective-permute-start.32 = (bf16[26,128,128]{2,1,0:T(8,128)(2,1)S(1)}, bf16[26,128,128]{2,1,0:T(8,128)(2,1)S(1)}, u32[]{:S(2)}, u32[]{:S(2)}) collective-permute-start(bf16[26,128,128]{2,1,0:T(8,128)(2,1)S(1)} %shard_map.67), channel_id=1, source_target_pairs={{0,1},{1,0},{2,3},{3,2},{4,5},{5,4},{6,7},{7,6},{8,9},{9,8},{10,11... | collective-permute-start | bytes 2555912 | tf_op jit(solution)/shard_map/ppermute | solution.py:33
  114.9 13.5 %collective-permute-start.24 = (bf16[128,1792]{1,0:T(8,128)(2,1)S(1)}, bf16[128,1792]{1,0:T(8,128)(2,1)S(1)}, u32[]{:S(2)}, u32[]{:S(2)}) collective-permute-start(bf16[128,1792]{1,0:T(8,128)(2,1)S(1)} %get-tuple-element.90), channel_id=1, source_target_pairs={{0,32},{1,33},{2,34},{3,35},{4,36},{5,37},{6,38},{7,39},{8,40},{9,... | collective-permute-start | bytes 1376264 | tf_op jit(solution)/shard_map/ppermute | solution.py:33
  115.2 14.7 %collective-permute-start.25 = (bf16[128,1792]{1,0:T(8,128)(2,1)S(1)}, bf16[128,1792]{1,0:T(8,128)(2,1)S(1)}, u32[]{:S(2)}, u32[]{:S(2)}) collective-permute-start(bf16[128,1792]{1,0:T(8,128)(2,1)S(1)} %get-tuple-element.96), channel_id=1, source_target_pairs={{0,96},{1,97},{2,98},{3,99},{4,100},{5,101},{6,102},{7,103},{8,104... | collective-permute-start | bytes 1376264 | tf_op jit(solution)/shard_map/ppermute | solution.py:33
  117.1 19.7 %collective-permute-start.28 = (bf16[128,1792]{1,0:T(8,128)(2,1)S(1)}, bf16[128,1792]{1,0:T(8,128)(2,1)S(1)}, u32[]{:S(2)}, u32[]{:S(2)}) collective-permute-start(bf16[128,1792]{1,0:T(8,128)(2,1)S(1)} %get-tuple-element.93), channel_id=1, source_target_pairs={{0,32},{1,33},{2,34},{3,35},{4,36},{5,37},{6,38},{7,39},{8,40},{9,... | collective-permute-start | bytes 1376264 | tf_op jit(solution)/shard_map/ppermute | solution.py:33
  118.7 19.3 %collective-permute-start.29 = (bf16[128,1792]{1,0:T(8,128)(2,1)S(1)}, bf16[128,1792]{1,0:T(8,128)(2,1)S(1)}, u32[]{:S(2)}, u32[]{:S(2)}) collective-permute-start(bf16[128,1792]{1,0:T(8,128)(2,1)S(1)} %get-tuple-element.102), channel_id=1, source_target_pairs={{0,96},{1,97},{2,98},{3,99},{4,100},{5,101},{6,102},{7,103},{8,104... | collective-permute-start | bytes 1376264 | tf_op jit(solution)/shard_map/ppermute | solution.py:33
  130.7 6.1 %collective-permute-start.26 = (bf16[128,896]{1,0:T(8,128)(2,1)S(1)}, bf16[128,896]{1,0:T(8,128)(2,1)S(1)}, u32[]{:S(2)}, u32[]{:S(2)}) collective-permute-start(bf16[128,896]{1,0:T(8,128)(2,1)S(1)} %get-tuple-element.98), channel_id=1, source_target_pairs={{0,1},{1,17},{2,3},{3,19},{4,5},{5,21},{6,7},{7,23},{8,9},{9,25},{... | collective-permute-start | bytes 688136 | tf_op jit(solution)/shard_map/ppermute | solution.py:33
  130.8 14.8 %collective-permute-start.27 = (bf16[128,896]{1,0:T(8,128)(2,1)S(1)}, bf16[128,896]{1,0:T(8,128)(2,1)S(1)}, u32[]{:S(2)}, u32[]{:S(2)}) collective-permute-start(bf16[128,896]{1,0:T(8,128)(2,1)S(1)} %get-tuple-element.99), channel_id=1, source_target_pairs={{1,16},{3,18},{5,20},{7,22},{9,24},{11,26},{13,28},{15,30},{16,1},... | collective-permute-start | bytes 688136 | tf_op jit(solution)/shard_map/ppermute | solution.py:33
  138.8 6.8 %collective-permute-start.30 = (bf16[128,896]{1,0:T(8,128)(2,1)S(1)}, bf16[128,896]{1,0:T(8,128)(2,1)S(1)}, u32[]{:S(2)}, u32[]{:S(2)}) collective-permute-start(bf16[128,896]{1,0:T(8,128)(2,1)S(1)} %get-tuple-element.104), channel_id=1, source_target_pairs={{0,1},{1,17},{2,3},{3,19},{4,5},{5,21},{6,7},{7,23},{8,9},{9,25},{... | collective-permute-start | bytes 688136 | tf_op jit(solution)/shard_map/ppermute | solution.py:33
  139.2 7.9 %collective-permute-start.31 = (bf16[128,896]{1,0:T(8,128)(2,1)S(1)}, bf16[128,896]{1,0:T(8,128)(2,1)S(1)}, u32[]{:S(2)}, u32[]{:S(2)}) collective-permute-start(bf16[128,896]{1,0:T(8,128)(2,1)S(1)} %get-tuple-element.105), channel_id=1, source_target_pairs={{1,16},{3,18},{5,20},{7,22},{9,24},{11,26},{13,28},{15,30},{16,1},... | collective-permute-start | bytes 688136 | tf_op jit(solution)/shard_map/ppermute | solution.py:33
